TPU v7x, 128 devices: a whole 4x4x4 slice. The times are simulated.
128 devices in a mesh: dap: 32 (over z_lo, y, x), rep: 4 (over z_hi, core).
Axes of the slice: x: 4, y: 4, z: 4 (z_hi: 2, z_lo: 2; z = z_hi * 2 + z_lo), core: 2. Of those that a mesh axis runs over, the one named last changes fastest.
Arguments:
- pair_state: bfloat16 [512, 512, 128], P(('dap', 'rep')), may hold values from -6 to 6
- input_weights: bfloat16 [2, 128, 512], replicated, may hold values from -0.5 to 0.5
- gate_weights: bfloat16 [2, 128, 128], replicated, may hold values from -0.5 to 0.5
- output_weights: bfloat16 [2, 128, 128], replicated, may hold values from -0.5 to 0.5
- input_gains: float32 [2, 128], replicated, may hold values from 0.25 to 1.75
- hidden_gains: float32 [2, 128], replicated, may hold values from 0.25 to 1.75
Outputs:
- updated: bfloat16 [512, 512, 128], P(None, ('dap', 'rep'))
All inputs are finite; a program needn't handle non-finite values.
Results may differ from a plain program's by a relative error of at most 0.012.
Values may be sent and summed in bfloat16 or wider, within the bound.
No kernel may reach another device: no remote copies, remote signals or barrier semaphores. Data moves between devices by JAX's collectives and lax.ppermute only.
A program may use at most 64 MiB of HBM per device.

v0:
```python
import jax
import jax.numpy as jnp
from jax import lax
from jax.sharding import PartitionSpec as P

epsilon = 1e-05


def normalize(values, scales, axis_index):
    average = jnp.mean(values, axis=axis_index, keepdims=True)
    centred = values - average
    variance = jnp.mean(centred * centred, axis=axis_index, keepdims=True)
    return centred * lax.rsqrt(variance + epsilon) * scales


def prepare(state, weights, scales):
    hidden = weights.shape[1] // 4
    normed = normalize(state.astype(jnp.float32), scales, 2).astype(jnp.bfloat16)
    pattern = "xyc,ch->xhy"
    outputs = []
    for half_index in range(2):
        linear = jnp.einsum(
            pattern,
            normed,
            weights[:, 2 * half_index * hidden : (2 * half_index + 1) * hidden],
            preferred_element_type=jnp.float32,
        )
        gating = jnp.einsum(
            pattern,
            normed,
            weights[:, (2 * half_index + 1) * hidden : (2 * half_index + 2) * hidden],
            preferred_element_type=jnp.float32,
        )
        outputs.append((jax.nn.sigmoid(gating) * linear).astype(jnp.bfloat16))
    return (normed, outputs[0], outputs[1])


def to_channels(left_side, right_side):
    return (
        lax.all_to_all(left_side, ("dap", "rep"), split_axis=1, concat_axis=0, tiled=True),
        lax.all_to_all(right_side, ("dap", "rep"), split_axis=1, concat_axis=0, tiled=True),
    )


def to_local(mixed):
    return lax.all_to_all(mixed, ("dap", "rep"), split_axis=0, concat_axis=1, tiled=True)


def finish(state, normed, mixed, gate_matrix, output_matrix, scales, layout):
    hidden_normed = normalize(mixed.astype(jnp.float32), scales[:, None], 1).astype(jnp.bfloat16)
    pattern = "xhy,hc->xyc" if layout == "rows" else "yhx,hc->xyc"
    update_term = jnp.einsum(
        pattern, hidden_normed, output_matrix, preferred_element_type=jnp.float32
    )
    gating = jax.nn.sigmoid(
        jnp.einsum("xyc,cd->xyd", normed, gate_matrix, preferred_element_type=jnp.float32)
    )
    return (state.astype(jnp.float32) + gating * update_term).astype(jnp.bfloat16)


def on_device(pair_state, input_weights, gate_weights, output_weights, input_gains, hidden_gains):
    normed, left_side, right_side = prepare(pair_state, input_weights[0], input_gains[0])
    left_all, right_all = to_channels(left_side, right_side)
    mixed = jnp.einsum(
        "igk,jgk->igj", left_all, right_all, preferred_element_type=jnp.float32
    ).astype(jnp.bfloat16)
    middle = finish(
        pair_state,
        normed,
        to_local(mixed),
        gate_weights[0],
        output_weights[0],
        hidden_gains[0],
        "rows",
    )
    left_side, right_side = prepare(middle, input_weights[1], input_gains[1])[1:]
    columns = lax.all_to_all(middle, ("dap", "rep"), split_axis=1, concat_axis=0, tiled=True)
    left_all, right_all = to_channels(left_side, right_side)
    mixed = jnp.einsum(
        "kgi,kgj->jgi", left_all, right_all, preferred_element_type=jnp.float32
    ).astype(jnp.bfloat16)
    normed = normalize(columns.astype(jnp.float32), input_gains[1], 2).astype(jnp.bfloat16)
    return finish(
        columns,
        normed,
        to_local(mixed),
        gate_weights[1],
        output_weights[1],
        hidden_gains[1],
        "cols",
    )


def solution(mesh):
    return jax.shard_map(
        on_device,
        mesh=mesh,
        in_specs=(P(("dap", "rep"), None, None), P(), P(), P(), P(), P()),
        out_specs=P(None, ("dap", "rep"), None),
        check_vma=False,
    )
```

profile of v0, /device:TPU:1, one launch (start us, length us, event | category | flops | bytes accessed | tf_op | source)
XLA Modules:
  0.0 157.7 jit_solution(3348299997329290974)
XLA Ops:
  0.0 1.2 copy.93
  3.2 1.2 copy.105
  4.4 11.5 %all-to-all-start.1 = ((bf16[4,128,512]{2,0,1:T(4,128)(2,1)}), bf16[4,128,512]{2,0,1:T(4,128)(2,1)S(1)}, u32[]{:S(2)}, u32[]{:S(2)}) async-start(bf16[4,128,512]{2,0,1:T(4,128)(2,1)} %copy.105), calls=%async_computation.1 | async-start | bytes 1048576 | tf_op jit(solution)/shard_map/all_to_all | solution.py:40
  16.9 1.2 copy.100
  18.1 11.3 %all-to-all-done.1 = bf16[4,128,512]{2,0,1:T(4,128)(2,1)S(1)} async-done(((bf16[4,128,512]{2,0,1:T(4,128)(2,1)}), bf16[4,128,512]{2,0,1:T(4,128)(2,1)S(1)}, u32[]{:S(2)}, u32[]{:S(2)}) %all-to-all-start.1) | async-done | bytes 524320 | tf_op jit(solution)/shard_map/all_to_all | solution.py:40
  29.3 4.7 %all-to-all-start = ((bf16[4,128,512]{2,0,1:T(4,128)(2,1)}), bf16[4,128,512]{2,0,1:T(4,128)(2,1)S(1)}, u32[]{:S(2)}, u32[]{:S(2)}) async-start(bf16[4,128,512]{2,0,1:T(4,128)(2,1)} %copy.100), calls=%async_computation | async-start | bytes 1048576 | tf_op jit(solution)/shard_map/all_to_all | solution.py:41
  34.2 13.3 %all-to-all-done = bf16[4,128,512]{2,0,1:T(4,128)(2,1)S(1)} async-done(((bf16[4,128,512]{2,0,1:T(4,128)(2,1)}), bf16[4,128,512]{2,0,1:T(4,128)(2,1)S(1)}, u32[]{:S(2)}, u32[]{:S(2)}) %all-to-all-start) | async-done | bytes 524320 | tf_op jit(solution)/shard_map/all_to_all | solution.py:41
  48.6 1.1 reduce.4
  49.9 1.1 reshape.142
  51.1 4.7 %all-to-all-start.2 = ((bf16[128,2,1024]{2,1,0:T(2,128)(2,1)}), bf16[128,2,1024]{2,1,0:T(2,128)(2,1)S(1)}, u32[]{:S(2)}, u32[]{:S(2)}) async-start(bf16[128,2,1024]{2,1,0:T(2,128)(2,1)} %reshape.142), calls=%async_computation.2 | async-start | bytes 1048576 | tf_op jit(solution)/shard_map/all_to_all | solution.py:46
  55.8 13.4 %all-to-all-done.2 = bf16[128,2,1024]{2,1,0:T(2,128)(2,1)S(1)} async-done(((bf16[128,2,1024]{2,1,0:T(2,128)(2,1)}), bf16[128,2,1024]{2,1,0:T(2,128)(2,1)S(1)}, u32[]{:S(2)}, u32[]{:S(2)}) %all-to-all-start.2) | async-done | bytes 524320 | tf_op jit(solution)/shard_map/all_to_all | solution.py:46
  69.6 1.1 convert_bitcast_fusion.1
  72.1 1.4 fusion.55
  74.9 1.1 copy.109
  76.0 4.7 %all-to-all-start.3 = ((bf16[4,512,128]{2,0,1:T(4,128)(2,1)}), bf16[4,512,128]{2,0,1:T(4,128)(2,1)S(1)}, u32[]{:S(2)}, u32[]{:S(2)}) async-start(bf16[4,512,128]{2,0,1:T(4,128)(2,1)} %copy.109), calls=%async_computation.3 | async-start | bytes 1048576 | tf_op jit(solution)/shard_map/all_to_all | solution.py:77
  81.8 1.2 copy.117
  83.0 11.1 %all-to-all-done.3 = bf16[4,512,128]{2,0,1:T(4,128)(2,1)S(1)} async-done(((bf16[4,512,128]{2,0,1:T(4,128)(2,1)}), bf16[4,512,128]{2,0,1:T(4,128)(2,1)S(1)}, u32[]{:S(2)}, u32[]{:S(2)}) %all-to-all-start.3) | async-done | bytes 524320 | tf_op jit(solution)/shard_map/all_to_all | solution.py:77
  94.1 4.7 %all-to-all-start.4 = ((bf16[4,128,512]{2,0,1:T(4,128)(2,1)}), bf16[4,128,512]{2,0,1:T(4,128)(2,1)S(1)}, u32[]{:S(2)}, u32[]{:S(2)}) async-start(bf16[4,128,512]{2,0,1:T(4,128)(2,1)} %copy.117), calls=%async_computation.4 | async-start | bytes 1048576 | tf_op jit(solution)/shard_map/all_to_all | solution.py:41
  99.7 1.2 copy.123
  101.6 10.6 %all-to-all-done.4 = bf16[4,128,512]{2,0,1:T(4,128)(2,1)S(1)} async-done(((bf16[4,128,512]{2,0,1:T(4,128)(2,1)}), bf16[4,128,512]{2,0,1:T(4,128)(2,1)S(1)}, u32[]{:S(2)}, u32[]{:S(2)}) %all-to-all-start.4) | async-done | bytes 524320 | tf_op jit(solution)/shard_map/all_to_all | solution.py:41
  112.2 4.7 %all-to-all-start.5 = ((bf16[4,128,512]{2,0,1:T(4,128)(2,1)}), bf16[4,128,512]{2,0,1:T(4,128)(2,1)S(1)}, u32[]{:S(2)}, u32[]{:S(2)}) async-start(bf16[4,128,512]{2,0,1:T(4,128)(2,1)} %copy.123), calls=%async_computation.5 | async-start | bytes 1048576 | tf_op jit(solution)/shard_map/all_to_all | solution.py:40
  117.4 1.3 multiply_reduce_fusion
  118.7 11.6 %all-to-all-done.5 = bf16[4,128,512]{2,0,1:T(4,128)(2,1)S(1)} async-done(((bf16[4,128,512]{2,0,1:T(4,128)(2,1)}), bf16[4,128,512]{2,0,1:T(4,128)(2,1)S(1)}, u32[]{:S(2)}, u32[]{:S(2)}) %all-to-all-start.5) | async-done | bytes 524320 | tf_op jit(solution)/shard_map/all_to_all | solution.py:40
  130.8 1.1 reduce.5
  131.9 1.1 reshape.144
  133.0 4.7 %all-to-all-start.6 = ((bf16[128,2,1024]{2,1,0:T(2,128)(2,1)}), bf16[128,2,1024]{2,1,0:T(2,128)(2,1)S(1)}, u32[]{:S(2)}, u32[]{:S(2)}) async-start(bf16[128,2,1024]{2,1,0:T(2,128)(2,1)} %reshape.144), calls=%async_computation.6 | async-start | bytes 1048576 | tf_op jit(solution)/shard_map/all_to_all | solution.py:46
  137.7 1.4 multiply_convert_fusion.1
  139.1 1.2 copy.112
  140.4 1.7 %copy.111 = f32[128,4,4,128]{3,1,0,2:T(4,128)} copy(f32[128,4,4,128]{3,2,0,1:T(4,128)S(1)} %convert_bitcast_fusion) | data formatting | bytes 2097152 | tf_op jit(solution)/shard_map/convert_element_type | solution.py:58
  142.0 9.1 %all-to-all-done.6 = bf16[128,2,1024]{2,1,0:T(2,128)(2,1)S(1)} async-done(((bf16[128,2,1024]{2,1,0:T(2,128)(2,1)}), bf16[128,2,1024]{2,1,0:T(2,128)(2,1)S(1)}, u32[]{:S(2)}, u32[]{:S(2)}) %all-to-all-start.6) | async-done | bytes 524320 | tf_op jit(solution)/shard_map/all_to_all | solution.py:46
  151.5 1.6 %fusion.90 = (f32[4,128,1,512]{3,2,0,1:T(1,128)S(1)}, f32[128,4,1,512]{3,2,1,0:T(1,128)S(1)}) fusion(bf16[512,1,512]{2,1,0:T(2,128)(2,1)S(1)} %reshape.145), kind=kLoop, calls=%fused_computation.128 | loop fusion | flops 262144 | bytes 2621440 | tf_op jit(solution)/shard_map/convert_element_type | solution.py:50
  156.5 1.2 copy.127
  (59 shorter events, 15.0 us)
Async XLA Ops:
  1.4 1.0 copy-start.2
  1.5 0.7 copy-start.4
  4.4 24.9 %all-to-all-start.1 = ((bf16[4,128,512]{2,0,1:T(4,128)(2,1)}), bf16[4,128,512]{2,0,1:T(4,128)(2,1)S(1)}, u32[]{:S(2)}, u32[]{:S(2)}) async-start(bf16[4,128,512]{2,0,1:T(4,128)(2,1)} %copy.105), calls=%async_computation.1 | async-start | bytes 1048576 | tf_op jit(solution)/shard_map/all_to_all | solution.py:40
  29.3 18.1 %all-to-all-start = ((bf16[4,128,512]{2,0,1:T(4,128)(2,1)}), bf16[4,128,512]{2,0,1:T(4,128)(2,1)S(1)}, u32[]{:S(2)}, u32[]{:S(2)}) async-start(bf16[4,128,512]{2,0,1:T(4,128)(2,1)} %copy.100), calls=%async_computation | async-start | bytes 1048576 | tf_op jit(solution)/shard_map/all_to_all | solution.py:41
  51.1 4.7 %copy-start.5 = (f32[2,128]{1,0:T(2,128)S(1)}, f32[2,128]{1,0:T(2,128)}, u32[]{:S(2)}) copy-start(f32[2,128]{1,0:T(2,128)} %param.11) | copy-start | bytes 3076
  51.1 18.1 %all-to-all-start.2 = ((bf16[128,2,1024]{2,1,0:T(2,128)(2,1)}), bf16[128,2,1024]{2,1,0:T(2,128)(2,1)S(1)}, u32[]{:S(2)}, u32[]{:S(2)}) async-start(bf16[128,2,1024]{2,1,0:T(2,128)(2,1)} %reshape.142), calls=%async_computation.2 | async-start | bytes 1048576 | tf_op jit(solution)/shard_map/all_to_all | solution.py:46
  72.1 1.5 copy-start.3
  73.5 0.8 copy-start.6
  76.0 18.1 %all-to-all-start.3 = ((bf16[4,512,128]{2,0,1:T(4,128)(2,1)}), bf16[4,512,128]{2,0,1:T(4,128)(2,1)S(1)}, u32[]{:S(2)}, u32[]{:S(2)}) async-start(bf16[4,512,128]{2,0,1:T(4,128)(2,1)} %copy.109), calls=%async_computation.3 | async-start | bytes 1048576 | tf_op jit(solution)/shard_map/all_to_all | solution.py:77
  94.1 18.1 %all-to-all-start.4 = ((bf16[4,128,512]{2,0,1:T(4,128)(2,1)}), bf16[4,128,512]{2,0,1:T(4,128)(2,1)S(1)}, u32[]{:S(2)}, u32[]{:S(2)}) async-start(bf16[4,128,512]{2,0,1:T(4,128)(2,1)} %copy.117), calls=%async_computation.4 | async-start | bytes 1048576 | tf_op jit(solution)/shard_map/all_to_all | solution.py:41
  112.2 18.1 %all-to-all-start.5 = ((bf16[4,128,512]{2,0,1:T(4,128)(2,1)}), bf16[4,128,512]{2,0,1:T(4,128)(2,1)S(1)}, u32[]{:S(2)}, u32[]{:S(2)}) async-start(bf16[4,128,512]{2,0,1:T(4,128)(2,1)} %copy.123), calls=%async_computation.5 | async-start | bytes 1048576 | tf_op jit(solution)/shard_map/all_to_all | solution.py:40
  133.0 18.1 %all-to-all-start.6 = ((bf16[128,2,1024]{2,1,0:T(2,128)(2,1)}), bf16[128,2,1024]{2,1,0:T(2,128)(2,1)S(1)}, u32[]{:S(2)}, u32[]{:S(2)}) async-start(bf16[128,2,1024]{2,1,0:T(2,128)(2,1)} %reshape.144), calls=%async_computation.6 | async-start | bytes 1048576 | tf_op jit(solution)/shard_map/all_to_all | solution.py:46
  154.7 1.2 copy-start
  154.7 1.4 copy-start.1
where the time goes:
time: 158 us
  waiting for transfers between devices  80.2 us (51%)
  starting transfers between devices  39.7 us (25%)
  local copies, waits for them, and re-layouts  18.3 us (12%)
  other arithmetic  12.3 us (8%)
  matrix products  6.77 us (4%)
    all_to_all x2, waiting for transfers between devices, to_channels(): lax.all_to_all(right_side, ('dap', 'rep'), split_axis=1, concat_axis=0, t...  23.8 us
    all_to_all x2, waiting for transfers between devices, to_channels(): lax.all_to_all(left_side, ('dap', 'rep'), split_axis=1, concat_axis=0, ti...  22.9 us
    all_to_all x2, waiting for transfers between devices, to_local(): lax.all_to_all(mixed, ('dap', 'rep'), split_axis=0, concat_axis=1, tiled=...  22.4 us
    all_to_all x2, starting transfers between devices, to_channels(): lax.all_to_all(left_side, ('dap', 'rep'), split_axis=1, concat_axis=0, ti...  16.2 us
    all_to_all x1, waiting for transfers between devices, on_device(): lax.all_to_all(middle, ('dap', 'rep'), split_axis=1, concat_axis=0, tiled...  11.1 us
    all_to_all x2, starting transfers between devices, to_local(): lax.all_to_all(mixed, ('dap', 'rep'), split_axis=0, concat_axis=1, tiled=...  9.4 us
    all_to_all x2, starting transfers between devices, to_channels(): lax.all_to_all(right_side, ('dap', 'rep'), split_axis=1, concat_axis=0, t...  9.4 us
    unnamed x20, local copies, waits for them, and re-layouts  6.29 us
  transfers between devices with their start and end apart: 7, of which 7 were waited for; matrix products, arithmetic and copies ran while one was open for 8% of the time, Pallas kernels for 0%

commit v1 on v0

v1 whole, which is shorter than its diff:
```python
import functools

import jax
import jax.numpy as jnp
from jax import lax
from jax.experimental import pallas as pl
from jax.experimental.pallas import tpu as pltpu
from jax.sharding import PartitionSpec as P

epsilon = 1e-05
AXES = ("dap", "rep")
F32 = jnp.float32
BF16 = jnp.bfloat16
LANES = 128
VMEM_LIMIT = 40 * 1024 * 1024


def dot_nn(a, b):
    return lax.dot_general(a, b, (((1,), (0,)), ((), ())), preferred_element_type=F32)


def dot_nt(a, b):
    return lax.dot_general(a, b, (((1,), (1,)), ((), ())), preferred_element_type=F32)


def half_sigmoid(x):
    return 0.5 * jnp.tanh(x) + 0.5


def norm_lanes(x, x16, ones, gain):
    cen = x - dot_nn(x16, ones)
    sq = cen * cen
    high = sq.astype(BF16)
    low = (sq - high.astype(F32)).astype(BF16)
    var = dot_nn(high, ones) + dot_nn(low, ones)
    return (cen * lax.rsqrt(var + epsilon) * gain).astype(BF16)


def norm_rows(x, gain):
    cen = x - jnp.mean(x, axis=0, keepdims=True)
    var = jnp.mean(cen * cen, axis=0, keepdims=True)
    return (cen * lax.rsqrt(var + epsilon) * gain).astype(BF16)


def store_operands(pt, index, left_s, right_s):
    ch = pt.shape[0] // 4
    chunks = pt.shape[1] // LANES
    left = half_sigmoid(pt[ch : 2 * ch]) * pt[:ch]
    right = half_sigmoid(pt[3 * ch :]) * pt[2 * ch : 3 * ch]
    for c in range(chunks):
        sl = pl.ds(index * chunks + c, ch, stride=16)
        left_s[sl, :] = left[:, c * LANES : (c + 1) * LANES]
        right_s[sl, :] = right[:, c * LANES : (c + 1) * LANES]


def prepare_kernel(x_ref, wt_ref, gain_ref, ones_ref, out_ref, left_s, right_s, state_s, x_s):
    rows, tokens, _ = x_ref.shape
    peers = out_ref.shape[0]
    cols = tokens // peers
    for i in range(rows):
        x16 = x_ref[i]
        x = x16.astype(F32)
        x_s[...] = x
        normed = norm_lanes(x, x16, ones_ref[...], gain_ref[...])
        store_operands(dot_nt(wt_ref[...], normed), i, left_s, right_s)
        for j in range(cols):
            state_s[pl.ds(i * cols + j, peers, stride=16), :] = x_s[pl.ds(j, peers, stride=cols), :]
    for part, ref in enumerate((left_s, right_s, state_s)):
        out_ref[:, 16 * part : 16 * (part + 1), :] = ref[...].reshape(peers, 16, LANES).astype(BF16)


def mix_kernel(in_ref, out_ref, left_s, right_s, left_b, right_b):
    peers = in_ref.shape[0]
    tokens = left_b.shape[0]
    chunks = tokens // LANES
    for part, (wide, whole) in enumerate(((left_s, left_b), (right_s, right_b))):
        wide[...] = in_ref[:, 16 * part : 16 * (part + 1), :].astype(F32).reshape(peers * 16, LANES)
        for c in range(chunks):
            whole[:, c * LANES : (c + 1) * LANES] = wide[pl.ds(c, tokens, stride=chunks), :].astype(BF16)
    for c in range(chunks):
        left_s[pl.ds(c, tokens, stride=chunks), :] = dot_nt(
            right_b[...], left_b[c * LANES : (c + 1) * LANES, :]
        )
    out_ref[...] = left_s[...].reshape(peers, 16, LANES).astype(BF16)


def gate_first_kernel(in_ref, gt_ref, gain_ref, ones_ref, state_ref, gate_ref, wide):
    peers = in_ref.shape[0]
    cols, _, tokens = state_ref.shape
    wide[...] = in_ref[:, 32:48, :].astype(F32).reshape(peers * 16, LANES)
    for j in range(cols):
        x = wide[pl.ds(j, tokens, stride=cols), :]
        normed = norm_lanes(x, x.astype(BF16), ones_ref[...], gain_ref[...])
        gate_ref[j] = half_sigmoid(dot_nt(gt_ref[...], normed))
        state_ref[j] = x.T.astype(BF16)


def gate_second_kernel(state_ref, gt_ref, gain_ref, gate_ref):
    for j in range(state_ref.shape[0]):
        normed = norm_rows(state_ref[j].astype(F32), gain_ref[...])
        gate_ref[j] = half_sigmoid(dot_nn(gt_ref[...], normed))


def normalize_mixed(mixed_ref, wide):
    y = mixed_ref[...].astype(F32)
    cen = y - jnp.mean(y, axis=0, keepdims=True)
    var = jnp.mean(cen * cen, axis=0, keepdims=True)
    wide[...] = (cen * lax.rsqrt(var + epsilon)).reshape(wide.shape)


def hidden_of(wide, j, chunks, gain):
    channels = gain.shape[0]
    return jnp.concatenate(
        [
            (wide[pl.ds(j * chunks + c, channels, stride=16), :] * gain).astype(BF16)
            for c in range(chunks)
        ],
        axis=1,
    )


def middle_kernel(
    mixed_ref, state_ref, gate_ref, hgain_ref, ot_ref, igain_ref, wt_ref, out_ref, next_ref, wide, left_s, right_s
):
    cols, _, tokens = state_ref.shape
    chunks = tokens // LANES
    peers = out_ref.shape[0]
    normalize_mixed(mixed_ref, wide)
    for j in range(cols):
        update = dot_nn(ot_ref[...], hidden_of(wide, j, chunks, hgain_ref[...]))
        state = (state_ref[j].astype(F32) + gate_ref[j] * update).astype(BF16)
        next_ref[j] = state
        normed = norm_rows(state.astype(F32), igain_ref[...])
        store_operands(dot_nn(wt_ref[...], normed), j, left_s, right_s)
    for part, ref in enumerate((left_s, right_s)):
        out_ref[:, 16 * part : 16 * (part + 1), :] = ref[...].reshape(peers, 16, LANES).astype(BF16)


def last_kernel(mixed_ref, state_ref, gate_ref, hgain_ref, ot_ref, out_ref, wide, out_s):
    cols, _, tokens = state_ref.shape
    chunks = tokens // LANES
    normalize_mixed(mixed_ref, wide)
    for j in range(cols):
        update = dot_nn(ot_ref[...], hidden_of(wide, j, chunks, hgain_ref[...]))
        state = state_ref[j].astype(F32) + gate_ref[j] * update
        out_s[pl.ds(j, tokens, stride=cols), :] = state.T
    out_ref[...] = out_s[...].astype(BF16)


def call(kernel, out_shape, scratch, flops, moved, *args):
    return pl.pallas_call(
        kernel,
        out_shape=out_shape,
        scratch_shapes=[pltpu.VMEM(shape, dtype) for shape, dtype in scratch],
        compiler_params=pltpu.CompilerParams(vmem_limit_bytes=VMEM_LIMIT),
        cost_estimate=pl.CostEstimate(flops=flops, bytes_accessed=moved, transcendentals=0),
    )(*args)


def exchange(buffer):
    return lax.all_to_all(buffer, AXES, split_axis=0, concat_axis=0, tiled=True)


def on_device(pair_state, input_weights, gate_weights, output_weights, input_gains, hidden_gains):
    rows, tokens, cp = pair_state.shape
    ch = output_weights.shape[1]
    peers = tokens // rows
    shape = jax.ShapeDtypeStruct
    positions = rows * tokens
    wide = ((positions, LANES), F32)
    whole = ((tokens, tokens), BF16)
    size = positions * ch * 2

    halves = jnp.repeat(jnp.array([1.0, 0.5, 1.0, 0.5], BF16), ch)[None, :, None]
    wt = jnp.swapaxes(input_weights, 1, 2) * halves
    gt = jnp.swapaxes(gate_weights, 1, 2) * jnp.array(0.5, BF16)
    ot = jnp.swapaxes(output_weights, 1, 2)
    gain_wide = input_gains[1][:, None]
    hidden_wide = hidden_gains[:, :, None]
    ones = jnp.full((cp, cp), 1.0 / cp, BF16)
    project = 2 * positions * cp * 4 * ch
    mixing = 2 * tokens**3
    small = 2 * positions * cp * ch

    sent = call(
        prepare_kernel,
        shape((peers, 48, LANES), BF16),
        [wide, wide, wide, ((tokens, cp), F32)],
        project,
        4 * size,
        pair_state,
        wt[0],
        input_gains[:1],
        ones,
    )
    got = exchange(sent)
    mix = functools.partial(
        call,
        mix_kernel,
        shape((peers, 16, LANES), BF16),
        [wide, wide, whole, whole],
        mixing,
        3 * size,
    )
    mixed = exchange(mix(got))
    transposed = shape((rows, cp, tokens), BF16)
    gating = shape((rows, cp, tokens), F32)
    state, gate = call(
        gate_first_kernel,
        (transposed, gating),
        [wide],
        2 * small,
        5 * size,
        got,
        gt[0],
        input_gains[:1],
        ones,
    )
    sent, state = call(
        middle_kernel,
        (shape((peers, 32, LANES), BF16), transposed),
        [wide, wide, wide],
        project + small,
        6 * size,
        mixed,
        state,
        gate,
        hidden_wide[0],
        ot[0],
        gain_wide,
        wt[1],
    )
    mixed = exchange(mix(exchange(sent)))
    gate = call(gate_second_kernel, gating, [], small, 3 * size, state, gt[1], gain_wide)
    out = call(
        last_kernel,
        shape((positions, cp), BF16),
        [wide, wide],
        small,
        5 * size,
        mixed,
        state,
        gate,
        hidden_wide[1],
        ot[1],
    )
    return out.reshape(tokens, rows, cp)


def solution(mesh):
    return jax.shard_map(
        on_device,
        mesh=mesh,
        in_specs=(P(AXES, None, None), P(), P(), P(), P(), P()),
        out_specs=P(None, AXES, None),
        check_vma=False,
    )
```

time: 158 us -> 112 us (0.71)
  waiting for transfers between devices: 80.2 us -> 47 us
  blocking collectives: 0 us -> 23.3 us
  starting transfers between devices: 39.7 us -> 21.3 us
  Pallas kernels: 0 us -> 14.6 us
  local copies, waits for them, and re-layouts: 18.3 us -> 5.09 us
  other arithmetic: 12.3 us -> 0.14 us
  matrix products: 6.77 us -> 0 us
    all_to_all x7 -> x3, waiting for transfers between devices: 80.2 us -> 47 us  [exchange(): return lax.all_to_all(buffer, AXES, split_axis=0, concat_axis=0, tiled=True)]
    all_to_all x0 -> x1, blocking collectives: none -> 23.3 us  [exchange(): return lax.all_to_all(buffer, AXES, split_axis=0, concat_axis=0, tiled=True)]
    all_to_all x7 -> x3, starting transfers between devices: 39.7 us -> 21.3 us  [exchange(): return lax.all_to_all(buffer, AXES, split_axis=0, concat_axis=0, tiled=True)]
    pallas_call x0 -> x7, Pallas kernels: none -> 14.6 us  [call(): pl.pallas_call(kernel, out_shape=out_shape, scratch_shapes=[pltpu.VMEM(sh...]
    convert_element_type x10 -> x0, local copies, waits for them, and re-layouts: 11.3 us -> none  [the longest x4 4.79 us: prepare(): outputs.append((jax.nn.sigmoid(gating) * linear).astype(jnp.bfloat16))]
    convert_element_type x7 -> x0, other arithmetic: 7.71 us -> none  [the longest x2 2.7 us: finish(): mixed.astype(jnp.float32)]
    dot_general x14 -> x0, matrix products: 6.77 us -> none  [the longest x4 2.06 us: prepare(): jnp.einsum(pattern, normed, weights[:, (2 * half_index + 1) * hidden:(2 *...]
    reduce_sum x9 -> x0, other arithmetic: 4.43 us -> none  [the longest x5 2.3 us: normalize(): variance = jnp.mean(centred * centred, axis=axis_index, keepdims=True)]
  transfers between devices with their start and end apart: 7 -> 3, of which waited for: 7 -> 3; matrix products, arithmetic and copies ran while one was open for 8% -> 1% of each run, Pallas kernels for 0% -> 2%
where the time goes in v1:
time: 112 us
  waiting for transfers between devices  47 us (42%)
  blocking collectives  23.3 us (21%)
  starting transfers between devices  21.3 us (19%)
  Pallas kernels  14.6 us (13%)
  local copies, waits for them, and re-layouts  5.09 us (5%)
    all_to_all x3, waiting for transfers between devices, exchange(): return lax.all_to_all(buffer, AXES, split_axis=0, concat_axis=0, tiled=True)  47 us
    all_to_all x1, blocking collectives, exchange(): return lax.all_to_all(buffer, AXES, split_axis=0, concat_axis=0, tiled=True)  23.3 us
    all_to_all x3, starting transfers between devices, exchange(): return lax.all_to_all(buffer, AXES, split_axis=0, concat_axis=0, tiled=True)  21.3 us
    pallas_call x7, Pallas kernels, call(): pl.pallas_call(kernel, out_shape=out_shape, scratch_shapes=[pltpu.VMEM(sh...  14.6 us
    unnamed x15, local copies, waits for them, and re-layouts  3.22 us
  transfers between devices with their start and end apart: 3, of which 3 were waited for; matrix products, arithmetic and copies ran while one was open for 1% of the time, Pallas kernels for 2%

profile of v1, /device:TPU:1, one launch (start us, length us, event | category | flops | bytes accessed | tf_op | source)
XLA Modules:
  0.0 111.7 jit_solution(6458878707323521242)
XLA Ops:
  0.0 0.8 slice_bitcast_fusion.7
  0.8 1.1 copy.8
  1.9 0.7 broadcast_bitcast_fusion
  2.6 0.1 multiply_bitcast_fusion
  2.8 0.0 copy-done
  2.8 3.9 %shard_map.73 = bf16[128,48,128]{2,1,0:T(8,128)(2,1)} custom-call(bf16[4,512,128]{2,1,0:T(8,128)(2,1)S(1)} %copy-done, bf16[512,128]{1,0:T(8,128)(2,1)S(1)} %get-tuple-element.14.wt_ref, f32[1,128]{1,0:T(1,128)S(1)} %get-tuple-element.22.gain_ref, bf16[128,128]{1,0:T(8,128)(2,1)S(1)} %broadcast_in_dim.8.ones_ref), custom_call_target="tpu_custom_call" | custom-call | flops 268435456 | bytes 2097152 | tf_op jit(solution)/shard_map/pallas_call | solution.py:151
  6.7 11.5 %all-to-all-start = ((bf16[128,48,128]{2,1,0:T(8,128)(2,1)}), bf16[128,48,128]{2,1,0:T(8,128)(2,1)S(1)}, u32[]{:S(2)}, u32[]{:S(2)}) async-start(bf16[128,48,128]{2,1,0:T(8,128)(2,1)} %shard_map.73), calls=%async_computation | async-start | bytes 3145728 | tf_op jit(solution)/shard_map/all_to_all | solution.py:161
  18.2 0.0 copy-done.3
  18.2 0.1 copy.9
  18.4 0.0 copy-start.5
  18.4 0.0 copy-start.4
  18.4 24.1 %all-to-all-done.in_ref = bf16[128,48,128]{2,1,0:T(8,128)(2,1)S(1)} async-done(((bf16[128,48,128]{2,1,0:T(8,128)(2,1)}), bf16[128,48,128]{2,1,0:T(8,128)(2,1)S(1)}, u32[]{:S(2)}, u32[]{:S(2)}) %all-to-all-start) | async-done | bytes 1572896 | tf_op jit(solution)/shard_map/all_to_all | solution.py:161
  42.5 1.7 %shard_map.74 = bf16[128,16,128]{2,1,0:T(8,128)(2,1)} custom-call(bf16[128,48,128]{2,1,0:T(8,128)(2,1)S(1)} %all-to-all-done.in_ref), custom_call_target="tpu_custom_call" | custom-call | flops 268435456 | bytes 1572864 | tf_op jit(solution)/shard_map/pallas_call | solution.py:151
  44.2 5.0 %all-to-all-start.1 = ((bf16[128,16,128]{2,1,0:T(8,128)(2,1)}), bf16[128,16,128]{2,1,0:T(8,128)(2,1)S(1)}, u32[]{:S(2)}, u32[]{:S(2)}) async-start(bf16[128,16,128]{2,1,0:T(8,128)(2,1)} %shard_map.74), calls=%async_computation.1 | async-start | bytes 1048576 | tf_op jit(solution)/shard_map/all_to_all | solution.py:161
  49.2 0.0 copy-done.5
  49.2 0.1 copy.12.igain_ref.gain_ref
  49.3 0.0 copy-done.4
  49.3 0.1 copy.10
  49.4 0.1 copy.11.hgain_ref
  49.6 1.9 %shard_map.75 = (bf16[4,128,512]{2,1,0:T(8,128)(2,1)S(1)}, f32[4,128,512]{2,1,0:T(8,128)S(1)}) custom-call(bf16[128,48,128]{2,1,0:T(8,128)(2,1)S(1)} %all-to-all-done.in_ref, bf16[128,128]{1,0:T(8,128)(2,1)S(1)} %get-tuple-element.18.gt_ref, f32[1,128]{1,0:T(1,128)S(1)} %get-tuple-element.22.gain_ref, bf16[128,128]{1,0:T(8,128)(2,1)S(1)} %broadcast_in_dim.8.ones_ref), custom_call_target="tpu_custom_call" | custom-call | flops 134217728 | bytes 2621440 | tf_op jit(solution)/shard_map/pallas_call | solution.py:151
  51.5 0.0 copy-start.1
  51.5 0.8 copy-done.1
  52.3 10.3 %all-to-all-done.1.mixed_ref = bf16[128,16,128]{2,1,0:T(8,128)(2,1)S(1)} async-done(((bf16[128,16,128]{2,1,0:T(8,128)(2,1)}), bf16[128,16,128]{2,1,0:T(8,128)(2,1)S(1)}, u32[]{:S(2)}, u32[]{:S(2)}) %all-to-all-start.1) | async-done | bytes 524320 | tf_op jit(solution)/shard_map/all_to_all | solution.py:161
  62.6 1.0 copy-done.2
  63.6 2.8 %shard_map.76 = (bf16[128,32,128]{2,1,0:T(8,128)(2,1)S(1)}, bf16[4,128,512]{2,1,0:T(8,128)(2,1)S(1)}) custom-call(bf16[128,16,128]{2,1,0:T(8,128)(2,1)S(1)} %all-to-all-done.1.mixed_ref, bf16[4,128,512]{2,1,0:T(8,128)(2,1)S(1)} %copy-done.2, f32[4,128,512]{2,1,0:T(8,128)S(1)} %get-tuple-element.10.gate_ref, f32[128,1]{1,0:T(8,128)S(1)} %copy.11.hgain_ref, ...), custom_call_target="tpu_custom_call" | custom-call | flops 335544320 | bytes 3145728 | tf_op jit(solution)/shard_map/pallas_call | solution.py:151
  66.4 23.3 %all_to_all.20.in_ref = bf16[128,32,128]{2,1,0:T(8,128)(2,1)S(1)} all-to-all(bf16[128,32,128]{2,1,0:T(8,128)(2,1)S(1)} %get-tuple-element.11), channel_id=1, replica_groups=mesh['dap'=32,'rep'=4] {'dap','rep'}, dimensions={0} | all-to-all | bytes 2097152 | tf_op jit(solution)/shard_map/all_to_all | solution.py:161
  89.7 1.7 %shard_map.77 = bf16[128,16,128]{2,1,0:T(8,128)(2,1)} custom-call(bf16[128,32,128]{2,1,0:T(8,128)(2,1)S(1)} %all_to_all.20.in_ref), custom_call_target="tpu_custom_call" | custom-call | flops 268435456 | bytes 1572864 | tf_op jit(solution)/shard_map/pallas_call | solution.py:151
  91.4 4.9 %all-to-all-start.3 = ((bf16[128,16,128]{2,1,0:T(8,128)(2,1)}), bf16[128,16,128]{2,1,0:T(8,128)(2,1)S(1)}, u32[]{:S(2)}, u32[]{:S(2)}) async-start(bf16[128,16,128]{2,1,0:T(8,128)(2,1)} %shard_map.77), calls=%async_computation.3 | async-start | bytes 1048576 | tf_op jit(solution)/shard_map/all_to_all | solution.py:161
  96.3 0.1 copy.14.hgain_ref
  96.4 0.6 shard_map.78.gate_ref
  97.0 12.7 %all-to-all-done.3.mixed_ref = bf16[128,16,128]{2,1,0:T(8,128)(2,1)S(1)} async-done(((bf16[128,16,128]{2,1,0:T(8,128)(2,1)}), bf16[128,16,128]{2,1,0:T(8,128)(2,1)S(1)}, u32[]{:S(2)}, u32[]{:S(2)}) %all-to-all-start.3) | async-done | bytes 524320 | tf_op jit(solution)/shard_map/all_to_all | solution.py:161
  109.7 2.0 %shard_map.79 = bf16[2048,128]{1,0:T(8,128)(2,1)} custom-call(bf16[128,16,128]{2,1,0:T(8,128)(2,1)S(1)} %all-to-all-done.3.mixed_ref, bf16[4,128,512]{2,1,0:T(8,128)(2,1)S(1)} %get-tuple-element.12.state_ref, f32[4,128,512]{2,1,0:T(8,128)S(1)} %shard_map.78.gate_ref, f32[128,1]{1,0:T(8,128)S(1)} %copy.14.hgain_ref, bf16[128,128]{1,0:T(8,128)(2,1)S(1)} %get-tuple-element.15.ot_ref), custom_call_target="tpu_custom_call" | custom-call | flops 67108864 | bytes 2621440 | tf_op jit(solution)/shard_map/pallas_call | solution.py:151
  (9 shorter events, 0.1 us)
Async XLA Ops:
  0.0 2.8 %copy-start = (bf16[4,512,128]{2,1,0:T(8,128)(2,1)S(1)}, bf16[4,512,128]{2,1,0:T(8,128)(2,1)}, u32[]{:S(2)}) copy-start(bf16[4,512,128]{2,1,0:T(8,128)(2,1)} %x_ref.1) | copy-start | bytes 1572868
  6.7 11.5 %copy-start.3 = (bf16[2,128,128]{2,1,0:T(8,128)(2,1)S(1)}, bf16[2,128,128]{2,1,0:T(8,128)(2,1)}, u32[]{:S(2)}) copy-start(bf16[2,128,128]{2,1,0:T(8,128)(2,1)} %param.9) | copy-start | bytes 196612
  6.7 35.8 %all-to-all-start = ((bf16[128,48,128]{2,1,0:T(8,128)(2,1)}), bf16[128,48,128]{2,1,0:T(8,128)(2,1)S(1)}, u32[]{:S(2)}, u32[]{:S(2)}) async-start(bf16[128,48,128]{2,1,0:T(8,128)(2,1)} %shard_map.73), calls=%async_computation | async-start | bytes 3145728 | tf_op jit(solution)/shard_map/all_to_all | solution.py:161
  18.4 30.8 %copy-start.5 = (f32[2,128]{1,0:T(2,128)S(1)}, f32[2,128]{1,0:T(2,128)}, u32[]{:S(2)}) copy-start(f32[2,128]{1,0:T(2,128)} %param.12) | copy-start | bytes 3076
  18.4 31.0 %copy-start.4 = (bf16[2,128,128]{2,1,0:T(8,128)(2,1)S(1)}, bf16[2,128,128]{2,1,0:T(8,128)(2,1)}, u32[]{:S(2)}) copy-start(bf16[2,128,128]{2,1,0:T(8,128)(2,1)} %param.10) | copy-start | bytes 196612
  44.2 18.4 %all-to-all-start.1 = ((bf16[128,16,128]{2,1,0:T(8,128)(2,1)}), bf16[128,16,128]{2,1,0:T(8,128)(2,1)S(1)}, u32[]{:S(2)}, u32[]{:S(2)}) async-start(bf16[128,16,128]{2,1,0:T(8,128)(2,1)} %shard_map.74), calls=%async_computation.1 | async-start | bytes 1048576 | tf_op jit(solution)/shard_map/all_to_all | solution.py:161
  51.5 0.8 copy-start.1
  62.6 1.0 copy-start.2
  91.4 18.3 %all-to-all-start.3 = ((bf16[128,16,128]{2,1,0:T(8,128)(2,1)}), bf16[128,16,128]{2,1,0:T(8,128)(2,1)S(1)}, u32[]{:S(2)}, u32[]{:S(2)}) async-start(bf16[128,16,128]{2,1,0:T(8,128)(2,1)} %shard_map.77), calls=%async_computation.3 | async-start | bytes 1048576 | tf_op jit(solution)/shard_map/all_to_all | solution.py:161

commit v2 on v1

v2 whole, which is shorter than its diff:
```python
import functools

import jax
import jax.numpy as jnp
from jax import lax
from jax.experimental import pallas as pl
from jax.experimental.pallas import tpu as pltpu
from jax.sharding import PartitionSpec as P

epsilon = 1e-05
AXES = ("dap", "rep")
F32 = jnp.float32
BF16 = jnp.bfloat16
LANES = 128
VMEM_LIMIT = 24 * 1024 * 1024


def dot_nn(a, b):
    return lax.dot_general(a, b, (((1,), (0,)), ((), ())), preferred_element_type=F32)


def dot_nt(a, b):
    return lax.dot_general(a, b, (((1,), (1,)), ((), ())), preferred_element_type=F32)


def half_sigmoid(x):
    return 0.5 * jnp.tanh(x) + 0.5


def norm_lanes(x, gain):
    cen = x - jnp.mean(x, axis=1, keepdims=True)
    var = jnp.mean(cen * cen, axis=1, keepdims=True)
    return (cen * lax.rsqrt(var + epsilon) * gain).astype(BF16)


def norm_wide(x, gain_ref):
    cen = x - jnp.mean(x, axis=0, keepdims=True)
    var = jnp.mean(cen * cen, axis=0, keepdims=True)
    unit = cen * lax.rsqrt(var + epsilon)
    return jnp.concatenate(
        [
            (unit[:, c : c + LANES] * gain_ref[...]).astype(BF16)
            for c in range(0, x.shape[1], LANES)
        ],
        axis=1,
    )


def store_operands(pt, index, left_s, right_s):
    ch = pt.shape[0] // 4
    chunks = pt.shape[1] // LANES
    left = half_sigmoid(pt[ch : 2 * ch]) * pt[:ch]
    right = half_sigmoid(pt[3 * ch :]) * pt[2 * ch : 3 * ch]
    for c in range(chunks):
        sl = pl.ds(index * chunks + c, ch, stride=16)
        left_s[sl, :] = left[:, c * LANES : (c + 1) * LANES]
        right_s[sl, :] = right[:, c * LANES : (c + 1) * LANES]


def flip(block, factor=1.0):
    return (block.astype(F32).T * factor).astype(BF16)


def flip_projections(w_ref, update, wt_ref):
    ch = w_ref.shape[2] // 4
    for part in range(4):
        block = w_ref[update, :, part * ch : (part + 1) * ch]
        wt_ref[part * ch : (part + 1) * ch, :] = flip(block, 0.5 if part % 2 else 1.0)


def widen(gain):
    return jnp.broadcast_to(gain, (LANES, gain.shape[1])).T


def prepare_kernel(x_ref, w_ref, gain_ref, out_ref, wt_s, left_s, right_s, state_s, x_s):
    rows, tokens, _ = x_ref.shape
    peers = out_ref.shape[0]
    cols = tokens // peers
    flip_projections(w_ref, 0, wt_s)
    for i in range(rows):
        x = x_ref[i].astype(F32)
        x_s[...] = x
        store_operands(dot_nt(wt_s[...], norm_lanes(x, gain_ref[0:1, :])), i, left_s, right_s)
        for j in range(cols):
            state_s[pl.ds(i * cols + j, peers, stride=16), :] = x_s[pl.ds(j, peers, stride=cols), :]
    for part, ref in enumerate((left_s, right_s, state_s)):
        out_ref[:, 16 * part : 16 * (part + 1), :] = ref[...].reshape(peers, 16, LANES).astype(BF16)


def mix_kernel(in_ref, out_ref, left_s, right_s, left_b, right_b):
    peers = in_ref.shape[0]
    tokens = left_b.shape[0]
    chunks = tokens // LANES
    for part, (wide, whole) in enumerate(((left_s, left_b), (right_s, right_b))):
        wide[...] = in_ref[:, 16 * part : 16 * (part + 1), :].astype(F32).reshape(peers * 16, LANES)
        for c in range(chunks):
            whole[:, c * LANES : (c + 1) * LANES] = wide[pl.ds(c, tokens, stride=chunks), :].astype(BF16)
    mixed = dot_nt(right_b[...], left_b[...])
    for c in range(chunks):
        left_s[pl.ds(c, tokens, stride=chunks), :] = mixed[:, c * LANES : (c + 1) * LANES]
    out_ref[...] = left_s[...].reshape(peers, 16, LANES).astype(BF16)


def gate_first_kernel(
    in_ref, w_ref, g_ref, o_ref, igain_ref, hgain_ref, state_ref, gate_ref, wt_ref, gt_ref, ot_ref, iwide_ref, hwide_ref, wide
):
    peers = in_ref.shape[0]
    cols, _, tokens = state_ref.shape
    wide[...] = in_ref[:, 32:48, :].astype(F32).reshape(peers * 16, LANES)
    first = flip(g_ref[0], 0.5)
    for j in range(cols):
        x = wide[pl.ds(j, tokens, stride=cols), :]
        normed = norm_lanes(x, igain_ref[0:1, :])
        gate_ref[j] = half_sigmoid(dot_nt(first, normed))
        state_ref[j] = x.T.astype(BF16)
    flip_projections(w_ref, 1, wt_ref)
    gt_ref[...] = flip(g_ref[1], 0.5)
    iwide_ref[...] = widen(igain_ref[1:2, :])
    for update in range(2):
        ot_ref[update] = flip(o_ref[update])
        hwide_ref[update] = widen(hgain_ref[update : update + 1, :])


def gate_second_kernel(state_ref, gt_ref, igain_ref, gate_ref):
    for j in range(state_ref.shape[0]):
        normed = norm_wide(state_ref[j].astype(F32), igain_ref)
        gate_ref[j] = half_sigmoid(dot_nn(gt_ref[...], normed))


def normalize_mixed(mixed_ref, wide):
    y = mixed_ref[...].astype(F32)
    cen = y - jnp.mean(y, axis=0, keepdims=True)
    var = jnp.mean(cen * cen, axis=0, keepdims=True)
    wide[...] = (cen * lax.rsqrt(var + epsilon)).reshape(wide.shape)


def hidden_of(wide, update, j, chunks, gain_ref):
    channels = gain_ref.shape[1]
    return jnp.concatenate(
        [
            (wide[pl.ds(j * chunks + c, channels, stride=16), :] * gain_ref[update]).astype(BF16)
            for c in range(chunks)
        ],
        axis=1,
    )


def middle_kernel(
    mixed_ref, state_ref, gate_ref, hgain_ref, ot_ref, igain_ref, wt_ref, out_ref, next_ref, wide, left_s, right_s
):
    cols, _, tokens = state_ref.shape
    chunks = tokens // LANES
    peers = out_ref.shape[0]
    normalize_mixed(mixed_ref, wide)
    for j in range(cols):
        update = dot_nn(ot_ref[0], hidden_of(wide, 0, j, chunks, hgain_ref))
        state = (state_ref[j].astype(F32) + gate_ref[j] * update).astype(BF16)
        next_ref[j] = state
        normed = norm_wide(state.astype(F32), igain_ref)
        store_operands(dot_nn(wt_ref[...], normed), j, left_s, right_s)
    for part, ref in enumerate((left_s, right_s)):
        out_ref[:, 16 * part : 16 * (part + 1), :] = ref[...].reshape(peers, 16, LANES).astype(BF16)


def last_kernel(mixed_ref, state_ref, gate_ref, hgain_ref, ot_ref, out_ref, wide, out_s):
    cols, _, tokens = state_ref.shape
    chunks = tokens // LANES
    normalize_mixed(mixed_ref, wide)
    for j in range(cols):
        update = dot_nn(ot_ref[1], hidden_of(wide, 1, j, chunks, hgain_ref))
        state = (state_ref[j].astype(F32) + gate_ref[j] * update).astype(BF16)
        out_s[pl.ds(j, tokens, stride=cols), :] = state.T.astype(F32)
    out_ref[...] = out_s[...].astype(BF16)


def call(kernel, out_shape, scratch, flops, moved, *args):
    return pl.pallas_call(
        kernel,
        out_shape=out_shape,
        scratch_shapes=[pltpu.VMEM(shape, dtype) for shape, dtype in scratch],
        compiler_params=pltpu.CompilerParams(vmem_limit_bytes=VMEM_LIMIT),
        cost_estimate=pl.CostEstimate(flops=flops, bytes_accessed=moved, transcendentals=0),
        name=kernel.__name__,
    )(*args)


def exchange(buffer):
    return lax.all_to_all(buffer, AXES, split_axis=0, concat_axis=0, tiled=True)


def on_device(pair_state, input_weights, gate_weights, output_weights, input_gains, hidden_gains):
    rows, tokens, cp = pair_state.shape
    ch = output_weights.shape[1]
    peers = tokens // rows
    shape = jax.ShapeDtypeStruct
    positions = rows * tokens
    wide = ((positions, LANES), F32)
    whole = ((tokens, tokens), BF16)
    size = positions * ch * 2
    project = 2 * positions * cp * 4 * ch
    small = 2 * positions * cp * ch
    mix = functools.partial(
        call,
        mix_kernel,
        shape((peers, 16, LANES), BF16),
        [wide, wide, whole, whole],
        2 * tokens**3,
        3 * size,
    )
    transposed = shape((rows, cp, tokens), BF16)
    gating = shape((rows, cp, tokens), F32)

    sent = call(
        prepare_kernel,
        shape((peers, 48, LANES), BF16),
        [((4 * ch, cp), BF16), wide, wide, wide, ((tokens, cp), F32)],
        project,
        4 * size,
        pair_state,
        input_weights,
        input_gains,
    )
    got = exchange(sent)
    mixed = exchange(mix(got))
    state, gate, wt, gt, ot, iwide, hwide = call(
        gate_first_kernel,
        (
            transposed,
            gating,
            shape((4 * ch, cp), BF16),
            shape((cp, cp), BF16),
            shape((2, cp, ch), BF16),
            shape((cp, LANES), F32),
            shape((2, ch, LANES), F32),
        ),
        [wide],
        2 * small,
        5 * size,
        got,
        input_weights,
        gate_weights,
        output_weights,
        input_gains,
        hidden_gains,
    )
    sent, state = call(
        middle_kernel,
        (shape((peers, 32, LANES), BF16), transposed),
        [wide, wide, wide],
        project + small,
        6 * size,
        mixed,
        state,
        gate,
        hwide,
        ot,
        iwide,
        wt,
    )
    mixed = exchange(mix(exchange(sent)))
    gate = call(gate_second_kernel, gating, [], small, 3 * size, state, gt, iwide)
    out = call(
        last_kernel,
        shape((positions, cp), BF16),
        [wide, wide],
        small,
        5 * size,
        mixed,
        state,
        gate,
        hwide,
        ot,
    )
    return out.reshape(tokens, rows, cp)


def solution(mesh):
    return jax.shard_map(
        on_device,
        mesh=mesh,
        in_specs=(P(AXES, None, None), P(), P(), P(), P(), P()),
        out_specs=P(None, AXES, None),
        check_vma=False,
    )
```

time: 112 us -> 112 us (level)
  blocking collectives: 23.3 us -> 58.9 us
  waiting for transfers between devices: 47 us -> 20 us
  starting transfers between devices: 21.3 us -> 9.84 us
  local copies, waits for them, and re-layouts: 5.09 us -> 11.3 us
  Pallas kernels: 14.6 us -> 11 us
    all_to_all x1 -> x2, blocking collectives: 23.3 us -> 58.9 us  [exchange(): return lax.all_to_all(buffer, AXES, split_axis=0, concat_axis=0, tiled=True)]
    all_to_all x3 -> x2, waiting for transfers between devices: 47 us -> 20 us  [exchange(): return lax.all_to_all(buffer, AXES, split_axis=0, concat_axis=0, tiled=True)]
    all_to_all x3 -> x2, starting transfers between devices: 21.3 us -> 9.84 us  [exchange(): return lax.all_to_all(buffer, AXES, split_axis=0, concat_axis=0, tiled=True)]
    unnamed x15 -> x40, local copies, waits for them, and re-layouts: 3.22 us -> 11.3 us
    pallas_call x7, Pallas kernels: 14.6 us -> 11 us  [call(): pl.pallas_call(kernel, out_shape=out_shape, scratch_shapes=[pltpu.VMEM(sh...]
  transfers between devices with their start and end apart: 3 -> 2, of which waited for: 3 -> 2; matrix products, arithmetic and copies ran while one was open for 1% -> 0% of each run, Pallas kernels for 2% -> 2%
where the time goes in v2:
time: 112 us; the launch traced here: 111 us
  blocking collectives  58.9 us (53%)
  waiting for transfers between devices  20 us (18%)
  local copies, waits for them, and re-layouts  11.3 us (10%)
  Pallas kernels  11 us (10%)
  starting transfers between devices  9.84 us (9%)
    all_to_all x2, blocking collectives, exchange(): return lax.all_to_all(buffer, AXES, split_axis=0, concat_axis=0, tiled=True)  58.9 us
    all_to_all x2, waiting for transfers between devices, exchange(): return lax.all_to_all(buffer, AXES, split_axis=0, concat_axis=0, tiled=True)  20 us
    unnamed x40, local copies, waits for them, and re-layouts  11.3 us
    pallas_call x7, Pallas kernels, call(): pl.pallas_call(kernel, out_shape=out_shape, scratch_shapes=[pltpu.VMEM(sh...  11 us
    all_to_all x2, starting transfers between devices, exchange(): return lax.all_to_all(buffer, AXES, split_axis=0, concat_axis=0, tiled=True)  9.84 us
  transfers between devices with their start and end apart: 2, of which 2 were waited for; matrix products, arithmetic and copies ran while one was open for 0% of the time, Pallas kernels for 2%

profile of v2, /device:TPU:1, one launch (start us, length us, event | category | flops | bytes accessed | tf_op | source)
XLA Modules:
  0.0 111.2 jit_solution(14866920209405326397)
XLA Ops:
  0.0 0.9 copy-done
  1.0 1.0 copy-done.4
  2.0 0.7 copy-done.17
  2.7 1.8 %prepare_kernel.1 = bf16[128,48,128]{2,1,0:T(8,128)(2,1)S(1)} custom-call(bf16[4,512,128]{2,1,0:T(8,128)(2,1)S(1)} %copy-done.4, bf16[2,128,512]{2,1,0:T(8,128)(2,1)S(1)} %copy-done, f32[2,128]{1,0:T(2,128)S(1)} %copy-done.17), custom_call_target="tpu_custom_call" | custom-call | flops 268435456 | bytes 2097152 | tf_op jit(solution)/shard_map/prepare_kernel/pallas_call | solution.py:177
  4.5 35.6 %all_to_all.20.in_ref = bf16[128,48,128]{2,1,0:T(8,128)(2,1)S(1)} all-to-all(bf16[128,48,128]{2,1,0:T(8,128)(2,1)S(1)} %prepare_kernel.1), channel_id=1, replica_groups=mesh['dap'=32,'rep'=4] {'dap','rep'}, dimensions={0} | all-to-all | bytes 3145728 | tf_op jit(solution)/shard_map/all_to_all | solution.py:188
  40.1 1.5 %mix_kernel.2 = bf16[128,16,128]{2,1,0:T(8,128)(2,1)} custom-call(bf16[128,48,128]{2,1,0:T(8,128)(2,1)S(1)} %all_to_all.20.in_ref), custom_call_target="tpu_custom_call" | custom-call | flops 268435456 | bytes 1572864 | tf_op jit(solution)/shard_map/mix_kernel/pallas_call | solution.py:177
  41.6 5.0 %all-to-all-start.1 = ((bf16[128,16,128]{2,1,0:T(8,128)(2,1)}), bf16[128,16,128]{2,1,0:T(8,128)(2,1)S(1)}, u32[]{:S(2)}, u32[]{:S(2)}) async-start(bf16[128,16,128]{2,1,0:T(8,128)(2,1)} %mix_kernel.2), calls=%async_computation.1 | async-start | bytes 1048576 | tf_op jit(solution)/shard_map/all_to_all | solution.py:188
  46.6 0.0 copy-done.1
  46.6 0.0 copy-done.18
  46.6 0.0 copy-done.19
  46.6 0.0 copy-start.13
  46.6 0.8 copy-done.13
  47.5 0.8 copy-done.14
  48.3 1.1 %gate_first_kernel.1 = (bf16[4,128,512]{2,1,0:T(8,128)(2,1)S(1)}, f32[4,128,512]{2,1,0:T(8,128)S(1)}, bf16[512,128]{1,0:T(8,128)(2,1)S(1)}, bf16[128,128]{1,0:T(...) custom-call(bf16[128,48,128]{2,1,0:T(8,128)(2,1)S(1)} %all_to_all.20.in_ref, ...), custom_call_target="tpu_custom_call" | custom-call | flops 134217728 | bytes 2621440 | tf_op jit(solution)/shard_map/gate_first_kernel/pallas_call | solution.py:177
  49.5 0.8 copy-done.2
  50.3 0.6 copy-done.5
  50.9 0.6 copy-done.8
  51.5 0.6 copy-done.11
  52.2 0.6 copy-done.15
  52.8 7.2 %all-to-all-done.1.mixed_ref = bf16[128,16,128]{2,1,0:T(8,128)(2,1)S(1)} async-done(((bf16[128,16,128]{2,1,0:T(8,128)(2,1)}), bf16[128,16,128]{2,1,0:T(8,128)(2,1)S(1)}, u32[]{:S(2)}, u32[]{:S(2)}) %all-to-all-start.1) | async-done | bytes 524320 | tf_op jit(solution)/shard_map/all_to_all | solution.py:188
  60.0 1.0 copy-done.3
  61.0 0.8 copy-done.6
  61.9 0.8 copy-done.9
  62.7 0.9 copy-done.12
  63.6 2.8 %middle_kernel.1 = (bf16[128,32,128]{2,1,0:T(8,128)(2,1)S(1)}, bf16[4,128,512]{2,1,0:T(8,128)(2,1)S(1)}) custom-call(bf16[128,16,128]{2,1,0:T(8,128)(2,1)S(1)} %all-to-all-done.1.mixed_ref, bf16[4,128,512]{2,1,0:T(8,128)(2,1)S(1)} %copy-done.3, f32[4,128,512]{2,1,0:T(8,128)S(1)} %get-tuple-element.15.gate_ref, ...), custom_call_target="tpu_custom_call" | custom-call | flops 335544320 | bytes 3145728 | tf_op jit(solution)/shard_map/middle_kernel/pallas_call | solution.py:177
  66.4 23.3 %all_to_all.21.in_ref = bf16[128,32,128]{2,1,0:T(8,128)(2,1)S(1)} all-to-all(bf16[128,32,128]{2,1,0:T(8,128)(2,1)S(1)} %get-tuple-element.20), channel_id=1, replica_groups=mesh['dap'=32,'rep'=4] {'dap','rep'}, dimensions={0} | all-to-all | bytes 2097152 | tf_op jit(solution)/shard_map/all_to_all | solution.py:188
  89.6 1.5 %mix_kernel.3 = bf16[128,16,128]{2,1,0:T(8,128)(2,1)} custom-call(bf16[128,32,128]{2,1,0:T(8,128)(2,1)S(1)} %all_to_all.21.in_ref), custom_call_target="tpu_custom_call" | custom-call | flops 268435456 | bytes 1572864 | tf_op jit(solution)/shard_map/mix_kernel/pallas_call | solution.py:177
  91.2 4.9 %all-to-all-start.3 = ((bf16[128,16,128]{2,1,0:T(8,128)(2,1)}), bf16[128,16,128]{2,1,0:T(8,128)(2,1)S(1)}, u32[]{:S(2)}, u32[]{:S(2)}) async-start(bf16[128,16,128]{2,1,0:T(8,128)(2,1)} %mix_kernel.3), calls=%async_computation.3 | async-start | bytes 1048576 | tf_op jit(solution)/shard_map/all_to_all | solution.py:188
  96.1 0.0 copy-done.10
  96.1 0.5 gate_second_kernel.1.gate_ref
  96.6 12.8 %all-to-all-done.3.mixed_ref = bf16[128,16,128]{2,1,0:T(8,128)(2,1)S(1)} async-done(((bf16[128,16,128]{2,1,0:T(8,128)(2,1)}), bf16[128,16,128]{2,1,0:T(8,128)(2,1)S(1)}, u32[]{:S(2)}, u32[]{:S(2)}) %all-to-all-start.3) | async-done | bytes 524320 | tf_op jit(solution)/shard_map/all_to_all | solution.py:188
  109.4 1.7 %last_kernel.1 = bf16[2048,128]{1,0:T(8,128)(2,1)} custom-call(bf16[128,16,128]{2,1,0:T(8,128)(2,1)S(1)} %all-to-all-done.3.mixed_ref, bf16[4,128,512]{2,1,0:T(8,128)(2,1)S(1)} %get-tuple-element.21.state_ref, f32[4,128,512]{2,1,0:T(8,128)S(1)} %gate_second_kernel.1.gate_ref, f32[2,128,128]{2,1,0:T(8,128)S(1)} %get-tuple-element.16.hgain_ref, ...), custom_call_target="tpu_custom_call" | custom-call | flops 67108864 | bytes 2621440 | tf_op jit(solution)/shard_map/last_kernel/pallas_call | solution.py:177
  (21 shorter events, 0.0 us)
Async XLA Ops:
  0.0 0.9 copy-start
  1.0 1.0 copy-start.4
  2.0 0.7 copy-start.17
  40.1 6.5 %copy-start.1 = (bf16[2,128,512]{2,1,0:T(8,128)(2,1)S(1)}, bf16[2,128,512]{2,1,0:T(8,128)(2,1)}, u32[]{:S(2)}) copy-start(bf16[2,128,512]{2,1,0:T(8,128)(2,1)} %w_ref.3) | copy-start | bytes 786436
  40.1 6.5 %copy-start.18 = (f32[2,128]{1,0:T(2,128)S(1)}, f32[2,128]{1,0:T(2,128)}, u32[]{:S(2)}) copy-start(f32[2,128]{1,0:T(2,128)} %igain_ref.1) | copy-start | bytes 3076
  40.1 6.5 %copy-start.19 = (f32[2,128]{1,0:T(2,128)S(1)}, f32[2,128]{1,0:T(2,128)}, u32[]{:S(2)}) copy-start(f32[2,128]{1,0:T(2,128)} %hgain_ref.1) | copy-start | bytes 3076
  41.6 18.4 %all-to-all-start.1 = ((bf16[128,16,128]{2,1,0:T(8,128)(2,1)}), bf16[128,16,128]{2,1,0:T(8,128)(2,1)S(1)}, u32[]{:S(2)}, u32[]{:S(2)}) async-start(bf16[128,16,128]{2,1,0:T(8,128)(2,1)} %mix_kernel.2), calls=%async_computation.1 | async-start | bytes 1048576 | tf_op jit(solution)/shard_map/all_to_all | solution.py:188
  46.6 0.8 copy-start.13
  47.5 0.8 copy-start.14
  49.4 0.8 copy-start.2
  50.3 0.6 copy-start.5
  50.9 0.6 copy-start.8
  51.5 0.7 copy-start.11
  52.2 0.6 copy-start.15
  60.0 1.0 copy-start.3
  61.0 0.8 copy-start.6
  61.9 0.8 copy-start.9
  62.7 0.9 copy-start.12
  89.6 6.4 %copy-start.10 = (f32[128,128]{1,0:T(8,128)S(1)}, f32[128,128]{1,0:T(8,128)}, u32[]{:S(2)}) copy-start(f32[128,128]{1,0:T(8,128)} %copy-done.8) | copy-start | bytes 196612
  89.6 6.4 %copy-start.16 = (bf16[128,128]{1,0:T(8,128)(2,1)S(1)}, bf16[128,128]{1,0:T(8,128)(2,1)}, u32[]{:S(2)}) copy-start(bf16[128,128]{1,0:T(8,128)(2,1)} %copy-done.15) | copy-start | bytes 98308
  91.2 18.3 %copy-start.7 = (bf16[2,128,128]{2,1,0:T(8,128)(2,1)S(1)}, bf16[2,128,128]{2,1,0:T(8,128)(2,1)}, u32[]{:S(2)}) copy-start(bf16[2,128,128]{2,1,0:T(8,128)(2,1)} %copy-done.5) | copy-start | bytes 196612
  91.2 18.3 %all-to-all-start.3 = ((bf16[128,16,128]{2,1,0:T(8,128)(2,1)}), bf16[128,16,128]{2,1,0:T(8,128)(2,1)S(1)}, u32[]{:S(2)}, u32[]{:S(2)}) async-start(bf16[128,16,128]{2,1,0:T(8,128)(2,1)} %mix_kernel.3), calls=%async_computation.3 | async-start | bytes 1048576 | tf_op jit(solution)/shard_map/all_to_all | solution.py:188

commit v3 on v2

--- a/solution.py
+++ b/solution.py
@@ -13,6 +13,7 @@
 BF16 = jnp.bfloat16
 LANES = 128
 VMEM_LIMIT = 24 * 1024 * 1024
+VMEM_SIZE = 64 * 1024 * 1024
 
 
 def dot_nn(a, b):
@@ -57,6 +58,21 @@
         right_s[sl, :] = right[:, c * LANES : (c + 1) * LANES]
 
 
+def send_out(parts, out_s, out_hbm, out_sem):
+    pieces = out_sem.shape[0]
+    size = out_s.shape[0] // pieces
+    copies = []
+    for p in range(pieces):
+        peers = slice(p * size, (p + 1) * size)
+        for part, ref in enumerate(parts):
+            block = ref[p * size * 16 : (p + 1) * size * 16, :]
+            out_s[peers, 16 * part : 16 * (part + 1), :] = block.reshape(size, 16, LANES).astype(BF16)
+        copies.append(pltpu.make_async_copy(out_s.at[peers], out_hbm.at[peers], out_sem.at[p]))
+        copies[-1].start()
+    for copy in copies:
+        copy.wait()
+
+
 def flip(block, factor=1.0):
     return (block.astype(F32).T * factor).astype(BF16)
 
@@ -72,22 +88,38 @@
     return jnp.broadcast_to(gain, (LANES, gain.shape[1])).T
 
 
-def prepare_kernel(x_ref, w_ref, gain_ref, out_ref, wt_s, left_s, right_s, state_s, x_s):
+def prepare_kernel(
+    x_hbm, w_hbm, gain_hbm, out_hbm, x_ref, w_ref, gain_ref, wt_s, left_s, right_s, state_s, x_s, out_s, x_sem, w_sem, gain_sem, out_sem
+):
     rows, tokens, _ = x_ref.shape
-    peers = out_ref.shape[0]
+    peers = out_s.shape[0]
     cols = tokens // peers
+    w_copy = pltpu.make_async_copy(w_hbm.at[0:1], w_ref, w_sem)
+    gain_copy = pltpu.make_async_copy(gain_hbm, gain_ref, gain_sem)
+    x_copies = [pltpu.make_async_copy(x_hbm.at[i], x_ref.at[i], x_sem.at[i]) for i in range(rows)]
+    w_copy.start()
+    gain_copy.start()
+    for copy in x_copies:
+        copy.start()
+    w_copy.wait()
     flip_projections(w_ref, 0, wt_s)
+    gain_copy.wait()
     for i in range(rows):
+        x_copies[i].wait()
         x = x_ref[i].astype(F32)
         x_s[...] = x
         store_operands(dot_nt(wt_s[...], norm_lanes(x, gain_ref[0:1, :])), i, left_s, right_s)
         for j in range(cols):
             state_s[pl.ds(i * cols + j, peers, stride=16), :] = x_s[pl.ds(j, peers, stride=cols), :]
-    for part, ref in enumerate((left_s, right_s, state_s)):
-        out_ref[:, 16 * part : 16 * (part + 1), :] = ref[...].reshape(peers, 16, LANES).astype(BF16)
-
-
-def mix_kernel(in_ref, out_ref, left_s, right_s, left_b, right_b):
+    send_out((left_s, right_s, state_s), out_s, out_hbm, out_sem)
+
+
+def mix_first_kernel(in_ref, out_hbm, state_ref, *scratch):
+    state_ref[...] = in_ref[:, 32:48, :]
+    mix_kernel(in_ref, out_hbm, *scratch)
+
+
+def mix_kernel(in_ref, out_hbm, left_s, right_s, left_b, right_b, out_s, out_sem):
     peers = in_ref.shape[0]
     tokens = left_b.shape[0]
     chunks = tokens // LANES
@@ -98,7 +130,7 @@
     mixed = dot_nt(right_b[...], left_b[...])
     for c in range(chunks):
         left_s[pl.ds(c, tokens, stride=chunks), :] = mixed[:, c * LANES : (c + 1) * LANES]
-    out_ref[...] = left_s[...].reshape(peers, 16, LANES).astype(BF16)
+    send_out((left_s,), out_s, out_hbm, out_sem)
 
 
 def gate_first_kernel(
@@ -106,7 +138,7 @@
 ):
     peers = in_ref.shape[0]
     cols, _, tokens = state_ref.shape
-    wide[...] = in_ref[:, 32:48, :].astype(F32).reshape(peers * 16, LANES)
+    wide[...] = in_ref[...].astype(F32).reshape(peers * 16, LANES)
     first = flip(g_ref[0], 0.5)
     for j in range(cols):
         x = wide[pl.ds(j, tokens, stride=cols), :]
@@ -173,14 +205,15 @@
     out_ref[...] = out_s[...].astype(BF16)
 
 
-def call(kernel, out_shape, scratch, flops, moved, *args):
+def call(kernel, out_shape, scratch, flops, moved, args, limit=VMEM_LIMIT, **options):
     return pl.pallas_call(
         kernel,
         out_shape=out_shape,
-        scratch_shapes=[pltpu.VMEM(shape, dtype) for shape, dtype in scratch],
-        compiler_params=pltpu.CompilerParams(vmem_limit_bytes=VMEM_LIMIT),
+        scratch_shapes=[pltpu.VMEM(*spec) if isinstance(spec, tuple) else spec for spec in scratch],
+        compiler_params=pltpu.CompilerParams(vmem_limit_bytes=limit),
         cost_estimate=pl.CostEstimate(flops=flops, bytes_accessed=moved, transcendentals=0),
         name=kernel.__name__,
+        **options,
     )(*args)
 
 
@@ -199,13 +232,12 @@
     size = positions * ch * 2
     project = 2 * positions * cp * 4 * ch
     small = 2 * positions * cp * ch
+    packed = shape((peers, 16, LANES), BF16)
     mix = functools.partial(
         call,
-        mix_kernel,
-        shape((peers, 16, LANES), BF16),
-        [wide, wide, whole, whole],
-        2 * tokens**3,
-        3 * size,
+        scratch=[wide, wide, whole, whole, ((peers, 16, LANES), BF16), pltpu.SemaphoreType.DMA((4,))],
+        flops=2 * tokens**3,
+        moved=3 * size,
     )
     transposed = shape((rows, cp, tokens), BF16)
     gating = shape((rows, cp, tokens), F32)
@@ -213,15 +245,33 @@
     sent = call(
         prepare_kernel,
         shape((peers, 48, LANES), BF16),
-        [((4 * ch, cp), BF16), wide, wide, wide, ((tokens, cp), F32)],
+        [
+            ((rows, tokens, cp), BF16),
+            ((1, cp, 4 * ch), BF16),
+            ((2, cp), F32),
+            ((4 * ch, cp), BF16),
+            wide,
+            wide,
+            wide,
+            ((tokens, cp), F32),
+            ((peers, 48, LANES), BF16),
+            pltpu.SemaphoreType.DMA((rows,)),
+            pltpu.SemaphoreType.DMA,
+            pltpu.SemaphoreType.DMA,
+            pltpu.SemaphoreType.DMA((4,)),
+        ],
         project,
         4 * size,
-        pair_state,
-        input_weights,
-        input_gains,
-    )
-    got = exchange(sent)
-    mixed = exchange(mix(got))
+        args=(pair_state, input_weights, input_gains),
+        limit=60 * 1024 * 1024,
+        in_specs=[pl.BlockSpec(memory_space=pltpu.HBM)] * 3,
+        out_specs=pl.BlockSpec(memory_space=pltpu.HBM),
+    )
+    in_hbm, in_vmem = (pl.BlockSpec(memory_space=m) for m in (pltpu.HBM, pltpu.VMEM))
+    mixed, state = mix(
+        mix_first_kernel, (packed, packed), args=(exchange(sent),), out_specs=(in_hbm, in_vmem)
+    )
+    mixed = exchange(mixed)
     state, gate, wt, gt, ot, iwide, hwide = call(
         gate_first_kernel,
         (
@@ -236,12 +286,7 @@
         [wide],
         2 * small,
         5 * size,
-        got,
-        input_weights,
-        gate_weights,
-        output_weights,
-        input_gains,
-        hidden_gains,
+        args=(state, input_weights, gate_weights, output_weights, input_gains, hidden_gains),
     )
     sent, state = call(
         middle_kernel,
@@ -249,27 +294,17 @@
         [wide, wide, wide],
         project + small,
         6 * size,
-        mixed,
-        state,
-        gate,
-        hwide,
-        ot,
-        iwide,
-        wt,
-    )
-    mixed = exchange(mix(exchange(sent)))
-    gate = call(gate_second_kernel, gating, [], small, 3 * size, state, gt, iwide)
+        args=(mixed, state, gate, hwide, ot, iwide, wt),
+    )
+    mixed = exchange(mix(mix_kernel, packed, args=(exchange(sent),), out_specs=in_hbm))
+    gate = call(gate_second_kernel, gating, [], small, 3 * size, (state, gt, iwide))
     out = call(
         last_kernel,
         shape((positions, cp), BF16),
         [wide, wide],
         small,
         5 * size,
-        mixed,
-        state,
-        gate,
-        hwide,
-        ot,
+        args=(mixed, state, gate, hwide, ot),
     )
     return out.reshape(tokens, rows, cp)
 

time: 112 us -> 108 us (0.964)
  local copies, waits for them, and re-layouts: 11.3 us -> 0.63 us
  waiting for transfers between devices: 20 us -> 24.4 us
  Pallas kernels: 11 us -> 14 us
    unnamed x40 -> x14, local copies, waits for them, and re-layouts: 11.3 us -> 0.63 us
    all_to_all x2, waiting for transfers between devices: 20 us -> 24.4 us  [exchange(): return lax.all_to_all(buffer, AXES, split_axis=0, concat_axis=0, tiled=True)]
    pallas_call x7, Pallas kernels: 11 us -> 14 us  [call(): pl.pallas_call(kernel, out_shape=out_shape, scratch_shapes=[pltpu.VMEM(*s...]
where the time goes in v3:
time: 108 us
  blocking collectives  59.1 us (55%)
  waiting for transfers between devices  24.4 us (23%)
  Pallas kernels  14 us (13%)
  starting transfers between devices  9.85 us (9%)
    all_to_all x2, blocking collectives, exchange(): return lax.all_to_all(buffer, AXES, split_axis=0, concat_axis=0, tiled=True)  59.1 us
    all_to_all x2, waiting for transfers between devices, exchange(): return lax.all_to_all(buffer, AXES, split_axis=0, concat_axis=0, tiled=True)  24.4 us
    pallas_call x7, Pallas kernels, call(): pl.pallas_call(kernel, out_shape=out_shape, scratch_shapes=[pltpu.VMEM(*s...  14 us
    all_to_all x2, starting transfers between devices, exchange(): return lax.all_to_all(buffer, AXES, split_axis=0, concat_axis=0, tiled=True)  9.85 us
  transfers between devices with their start and end apart: 2, of which 2 were waited for; matrix products, arithmetic and copies ran while one was open for 0% of the time, Pallas kernels for 2%

profile of v3, /device:TPU:1, one launch (start us, length us, event | category | flops | bytes accessed | tf_op | source)
XLA Modules:
  0.0 108.1 jit_solution(10604600531235631250)
XLA Ops:
  0.0 5.0 %prepare_kernel.1 = bf16[128,48,128]{2,1,0:T(8,128)(2,1)} custom-call(bf16[4,512,128]{2,1,0:T(8,128)(2,1)} %x_hbm.1, bf16[2,128,512]{2,1,0:T(8,128)(2,1)} %w_ref.1, f32[2,128]{1,0:T(2,128)} %igain_ref.1), custom_call_target="tpu_custom_call" | custom-call | flops 268435456 | bytes 2097152 | tf_op jit(solution)/shard_map/prepare_kernel/pallas_call | solution.py:209
  5.0 35.8 %all_to_all.20.in_ref = bf16[128,48,128]{2,1,0:T(8,128)(2,1)S(1)} all-to-all(bf16[128,48,128]{2,1,0:T(8,128)(2,1)} %prepare_kernel.1), channel_id=1, replica_groups=mesh['dap'=32,'rep'=4] {'dap','rep'}, dimensions={0} | all-to-all | bytes 3145728 | tf_op jit(solution)/shard_map/all_to_all | solution.py:221
  40.8 0.0 copy-start
  40.8 0.0 copy-start.1
  40.8 0.0 copy-start.2
  40.8 0.0 copy-start.5
  40.8 0.0 copy-start.6
  40.8 1.4 %mix_first_kernel.1 = (bf16[128,16,128]{2,1,0:T(8,128)(2,1)}, bf16[128,16,128]{2,1,0:T(8,128)(2,1)S(1)}) custom-call(bf16[128,48,128]{2,1,0:T(8,128)(2,1)S(1)} %all_to_all.20.in_ref), custom_call_target="tpu_custom_call" | custom-call | flops 268435456 | bytes 1572864 | tf_op jit(solution)/shard_map/mix_first_kernel/pallas_call | solution.py:209
  42.2 5.0 %all-to-all-start.1 = ((bf16[128,16,128]{2,1,0:T(8,128)(2,1)}), bf16[128,16,128]{2,1,0:T(8,128)(2,1)S(1)}, u32[]{:S(2)}, u32[]{:S(2)}) async-start(bf16[128,16,128]{2,1,0:T(8,128)(2,1)} %get-tuple-element.16), calls=%async_computation.1 | async-start | bytes 1048576 | tf_op jit(solution)/shard_map/all_to_all | solution.py:221
  47.2 0.0 copy-done
  47.2 0.0 copy-done.1
  47.2 0.0 copy-done.2
  47.2 0.0 copy-done.5
  47.3 0.0 copy-done.6
  47.3 1.1 %gate_first_kernel.1 = (bf16[4,128,512]{2,1,0:T(8,128)(2,1)S(1)}, f32[4,128,512]{2,1,0:T(8,128)S(1)}, bf16[512,128]{1,0:T(8,128)(2,1)S(1)}, bf16[128,128]{1,0:T(...) custom-call(bf16[128,16,128]{2,1,0:T(8,128)(2,1)S(1)} %get-tuple-element.17.in, ...), custom_call_target="tpu_custom_call" | custom-call | flops 134217728 | bytes 2621440 | tf_op jit(solution)/shard_map/gate_first_kernel/pallas_call | solution.py:209
  48.4 0.0 copy-start.3
  48.4 0.6 copy-done.3
  49.0 11.6 %all-to-all-done.1.mixed_ref = bf16[128,16,128]{2,1,0:T(8,128)(2,1)S(1)} async-done(((bf16[128,16,128]{2,1,0:T(8,128)(2,1)}), bf16[128,16,128]{2,1,0:T(8,128)(2,1)S(1)}, u32[]{:S(2)}, u32[]{:S(2)}) %all-to-all-start.1) | async-done | bytes 524320 | tf_op jit(solution)/shard_map/all_to_all | solution.py:221
  60.6 2.8 %middle_kernel.1 = (bf16[128,32,128]{2,1,0:T(8,128)(2,1)S(1)}, bf16[4,128,512]{2,1,0:T(8,128)(2,1)S(1)}) custom-call(bf16[128,16,128]{2,1,0:T(8,128)(2,1)S(1)} %all-to-all-done.1.mixed_ref, bf16[4,128,512]{2,1,0:T(8,128)(2,1)S(1)} %get-tuple-element.18.state_ref, f32[4,128,512]{2,1,0:T(8,128)S(1)} %get-tuple-element.19.gate_ref, ...), custom_call_target="tpu_custom_call" | custom-call | flops 335544320 | bytes 3145728 | tf_op jit(solution)/shard_map/middle_kernel/pallas_call | solution.py:209
  63.4 23.3 %all_to_all.21.in_ref = bf16[128,32,128]{2,1,0:T(8,128)(2,1)S(1)} all-to-all(bf16[128,32,128]{2,1,0:T(8,128)(2,1)S(1)} %get-tuple-element.24), channel_id=1, replica_groups=mesh['dap'=32,'rep'=4] {'dap','rep'}, dimensions={0} | all-to-all | bytes 2097152 | tf_op jit(solution)/shard_map/all_to_all | solution.py:221
  86.6 0.0 copy-start.4
  86.6 1.4 %mix_kernel.1 = bf16[128,16,128]{2,1,0:T(8,128)(2,1)} custom-call(bf16[128,32,128]{2,1,0:T(8,128)(2,1)S(1)} %all_to_all.21.in_ref), custom_call_target="tpu_custom_call" | custom-call | flops 268435456 | bytes 1572864 | tf_op jit(solution)/shard_map/mix_kernel/pallas_call | solution.py:209
  88.0 4.9 %all-to-all-start.3 = ((bf16[128,16,128]{2,1,0:T(8,128)(2,1)}), bf16[128,16,128]{2,1,0:T(8,128)(2,1)S(1)}, u32[]{:S(2)}, u32[]{:S(2)}) async-start(bf16[128,16,128]{2,1,0:T(8,128)(2,1)} %mix_kernel.1), calls=%async_computation.3 | async-start | bytes 1048576 | tf_op jit(solution)/shard_map/all_to_all | solution.py:221
  92.9 0.0 copy-done.4
  93.0 0.5 gate_second_kernel.1.gate_ref
  93.5 12.8 %all-to-all-done.3.mixed_ref = bf16[128,16,128]{2,1,0:T(8,128)(2,1)S(1)} async-done(((bf16[128,16,128]{2,1,0:T(8,128)(2,1)}), bf16[128,16,128]{2,1,0:T(8,128)(2,1)S(1)}, u32[]{:S(2)}, u32[]{:S(2)}) %all-to-all-start.3) | async-done | bytes 524320 | tf_op jit(solution)/shard_map/all_to_all | solution.py:221
  106.3 1.7 %last_kernel.1 = bf16[2048,128]{1,0:T(8,128)(2,1)} custom-call(bf16[128,16,128]{2,1,0:T(8,128)(2,1)S(1)} %all-to-all-done.3.mixed_ref, bf16[4,128,512]{2,1,0:T(8,128)(2,1)S(1)} %get-tuple-element.25.state_ref, f32[4,128,512]{2,1,0:T(8,128)S(1)} %gate_second_kernel.1.gate_ref, f32[2,128,128]{2,1,0:T(8,128)S(1)} %get-tuple-element.20.hgain_ref, ...), custom_call_target="tpu_custom_call" | custom-call | flops 67108864 | bytes 2621440 | tf_op jit(solution)/shard_map/last_kernel/pallas_call | solution.py:209
Async XLA Ops:
  40.8 6.4 %copy-start = (bf16[2,128,512]{2,1,0:T(8,128)(2,1)S(1)}, bf16[2,128,512]{2,1,0:T(8,128)(2,1)}, u32[]{:S(2)}) copy-start(bf16[2,128,512]{2,1,0:T(8,128)(2,1)} %w_ref.1) | copy-start | bytes 786436
  40.8 6.4 %copy-start.1 = (bf16[2,128,128]{2,1,0:T(8,128)(2,1)S(1)}, bf16[2,128,128]{2,1,0:T(8,128)(2,1)}, u32[]{:S(2)}) copy-start(bf16[2,128,128]{2,1,0:T(8,128)(2,1)} %g_ref.1) | copy-start | bytes 196612
  40.8 6.4 %copy-start.2 = (bf16[2,128,128]{2,1,0:T(8,128)(2,1)S(1)}, bf16[2,128,128]{2,1,0:T(8,128)(2,1)}, u32[]{:S(2)}) copy-start(bf16[2,128,128]{2,1,0:T(8,128)(2,1)} %o_ref.1) | copy-start | bytes 196612
  40.8 6.5 %copy-start.5 = (f32[2,128]{1,0:T(2,128)S(1)}, f32[2,128]{1,0:T(2,128)}, u32[]{:S(2)}) copy-start(f32[2,128]{1,0:T(2,128)} %igain_ref.1) | copy-start | bytes 3076
  40.8 6.5 %copy-start.6 = (f32[2,128]{1,0:T(2,128)S(1)}, f32[2,128]{1,0:T(2,128)}, u32[]{:S(2)}) copy-start(f32[2,128]{1,0:T(2,128)} %hgain_ref.1) | copy-start | bytes 3076
  42.2 18.4 %all-to-all-start.1 = ((bf16[128,16,128]{2,1,0:T(8,128)(2,1)}), bf16[128,16,128]{2,1,0:T(8,128)(2,1)S(1)}, u32[]{:S(2)}, u32[]{:S(2)}) async-start(bf16[128,16,128]{2,1,0:T(8,128)(2,1)} %get-tuple-element.16), calls=%async_computation.1 | async-start | bytes 1048576 | tf_op jit(solution)/shard_map/all_to_all | solution.py:221
  48.4 0.6 copy-start.3
  86.6 6.3 %copy-start.4 = (bf16[128,128]{1,0:T(8,128)(2,1)S(1)}, bf16[128,128]{1,0:T(8,128)(2,1)}, u32[]{:S(2)}) copy-start(bf16[128,128]{1,0:T(8,128)(2,1)} %copy-done.3) | copy-start | bytes 98308
  88.0 18.3 %all-to-all-start.3 = ((bf16[128,16,128]{2,1,0:T(8,128)(2,1)}), bf16[128,16,128]{2,1,0:T(8,128)(2,1)S(1)}, u32[]{:S(2)}, u32[]{:S(2)}) async-start(bf16[128,16,128]{2,1,0:T(8,128)(2,1)} %mix_kernel.1), calls=%async_computation.3 | async-start | bytes 1048576 | tf_op jit(solution)/shard_map/all_to_all | solution.py:221

commit v4 on v3

--- a/solution.py
+++ b/solution.py
@@ -13,7 +13,6 @@
 BF16 = jnp.bfloat16
 LANES = 128
 VMEM_LIMIT = 24 * 1024 * 1024
-VMEM_SIZE = 64 * 1024 * 1024
 
 
 def dot_nn(a, b):
@@ -56,6 +55,12 @@
         sl = pl.ds(index * chunks + c, ch, stride=16)
         left_s[sl, :] = left[:, c * LANES : (c + 1) * LANES]
         right_s[sl, :] = right[:, c * LANES : (c + 1) * LANES]
+
+
+def round_out(parts, out_ref):
+    for part, ref in enumerate(parts):
+        block = ref[...].reshape(out_ref.shape[0], 16, LANES)
+        out_ref[:, 16 * part : 16 * (part + 1), :] = block.astype(BF16)
 
 
 def send_out(parts, out_s, out_hbm, out_sem):
@@ -89,10 +94,10 @@
 
 
 def prepare_kernel(
-    x_hbm, w_hbm, gain_hbm, out_hbm, x_ref, w_ref, gain_ref, wt_s, left_s, right_s, state_s, x_s, out_s, x_sem, w_sem, gain_sem, out_sem
+    x_hbm, w_hbm, gain_hbm, out_ref, x_ref, w_ref, gain_ref, wt_s, left_s, right_s, state_s, x_s, x_sem, w_sem, gain_sem
 ):
     rows, tokens, _ = x_ref.shape
-    peers = out_s.shape[0]
+    peers = out_ref.shape[0]
     cols = tokens // peers
     w_copy = pltpu.make_async_copy(w_hbm.at[0:1], w_ref, w_sem)
     gain_copy = pltpu.make_async_copy(gain_hbm, gain_ref, gain_sem)
@@ -111,7 +116,7 @@
         store_operands(dot_nt(wt_s[...], norm_lanes(x, gain_ref[0:1, :])), i, left_s, right_s)
         for j in range(cols):
             state_s[pl.ds(i * cols + j, peers, stride=16), :] = x_s[pl.ds(j, peers, stride=cols), :]
-    send_out((left_s, right_s, state_s), out_s, out_hbm, out_sem)
+    round_out((left_s, right_s, state_s), out_ref)
 
 
 def mix_first_kernel(in_ref, out_hbm, state_ref, *scratch):
@@ -182,7 +187,6 @@
 ):
     cols, _, tokens = state_ref.shape
     chunks = tokens // LANES
-    peers = out_ref.shape[0]
     normalize_mixed(mixed_ref, wide)
     for j in range(cols):
         update = dot_nn(ot_ref[0], hidden_of(wide, 0, j, chunks, hgain_ref))
@@ -190,8 +194,7 @@
         next_ref[j] = state
         normed = norm_wide(state.astype(F32), igain_ref)
         store_operands(dot_nn(wt_ref[...], normed), j, left_s, right_s)
-    for part, ref in enumerate((left_s, right_s)):
-        out_ref[:, 16 * part : 16 * (part + 1), :] = ref[...].reshape(peers, 16, LANES).astype(BF16)
+    round_out((left_s, right_s), out_ref)
 
 
 def last_kernel(mixed_ref, state_ref, gate_ref, hgain_ref, ot_ref, out_ref, wide, out_s):
@@ -242,6 +245,7 @@
     transposed = shape((rows, cp, tokens), BF16)
     gating = shape((rows, cp, tokens), F32)
 
+    in_hbm, in_vmem = (pl.BlockSpec(memory_space=m) for m in (pltpu.HBM, pltpu.VMEM))
     sent = call(
         prepare_kernel,
         shape((peers, 48, LANES), BF16),
@@ -254,20 +258,18 @@
             wide,
             wide,
             ((tokens, cp), F32),
-            ((peers, 48, LANES), BF16),
             pltpu.SemaphoreType.DMA((rows,)),
             pltpu.SemaphoreType.DMA,
             pltpu.SemaphoreType.DMA,
-            pltpu.SemaphoreType.DMA((4,)),
         ],
         project,
         4 * size,
-        args=(pair_state, input_weights, input_gains),
-        limit=60 * 1024 * 1024,
-        in_specs=[pl.BlockSpec(memory_space=pltpu.HBM)] * 3,
-        out_specs=pl.BlockSpec(memory_space=pltpu.HBM),
-    )
-    in_hbm, in_vmem = (pl.BlockSpec(memory_space=m) for m in (pltpu.HBM, pltpu.VMEM))
+        args=[
+            pltpu.with_memory_space_constraint(a, pltpu.HBM)
+            for a in (pair_state, input_weights, input_gains)
+        ],
+        in_specs=[in_hbm] * 3,
+    )
     mixed, state = mix(
         mix_first_kernel, (packed, packed), args=(exchange(sent),), out_specs=(in_hbm, in_vmem)
     )

time: 108 us -> 107 us (level)
  Pallas kernels: 14 us -> 12.9 us
    pallas_call x7, Pallas kernels: 14 us -> 12.9 us  [call(): pl.pallas_call(kernel, out_shape=out_shape, scratch_shapes=[pltpu.VMEM(*s...]
where the time goes in v4:
time: 107 us
  blocking collectives  58.9 us (55%)
  waiting for transfers between devices  24.4 us (23%)
  Pallas kernels  12.9 us (12%)
  starting transfers between devices  9.85 us (9%)
    all_to_all x2, blocking collectives, exchange(): return lax.all_to_all(buffer, AXES, split_axis=0, concat_axis=0, tiled=True)  58.9 us
    all_to_all x2, waiting for transfers between devices, exchange(): return lax.all_to_all(buffer, AXES, split_axis=0, concat_axis=0, tiled=True)  24.4 us
    pallas_call x7, Pallas kernels, call(): pl.pallas_call(kernel, out_shape=out_shape, scratch_shapes=[pltpu.VMEM(*s...  12.9 us
    all_to_all x2, starting transfers between devices, exchange(): return lax.all_to_all(buffer, AXES, split_axis=0, concat_axis=0, tiled=True)  9.85 us
  transfers between devices with their start and end apart: 2, of which 2 were waited for; matrix products, arithmetic and copies ran while one was open for 0% of the time, Pallas kernels for 2%

profile of v4, /device:TPU:1, one launch (start us, length us, event | category | flops | bytes accessed | tf_op | source)
XLA Modules:
  0.0 106.8 jit_solution(16236427291235199190)
XLA Ops:
  0.0 3.9 %prepare_kernel.1 = bf16[128,48,128]{2,1,0:T(8,128)(2,1)S(1)} custom-call(bf16[4,512,128]{2,1,0:T(8,128)(2,1)} %x_hbm.1, bf16[2,128,512]{2,1,0:T(8,128)(2,1)} %w_ref.1, f32[2,128]{1,0:T(2,128)} %igain_ref.1), custom_call_target="tpu_custom_call" | custom-call | flops 268435456 | bytes 2097152 | tf_op jit(solution)/shard_map/prepare_kernel/pallas_call | solution.py:212
  3.9 35.6 %all_to_all.20.in_ref = bf16[128,48,128]{2,1,0:T(8,128)(2,1)S(1)} all-to-all(bf16[128,48,128]{2,1,0:T(8,128)(2,1)S(1)} %prepare_kernel.1), channel_id=1, replica_groups=mesh['dap'=32,'rep'=4] {'dap','rep'}, dimensions={0} | all-to-all | bytes 3145728 | tf_op jit(solution)/shard_map/all_to_all | solution.py:224
  39.5 0.0 copy-start
  39.5 0.0 copy-start.1
  39.5 0.0 copy-start.2
  39.5 0.0 copy-start.5
  39.5 0.0 copy-start.6
  39.5 1.4 %mix_first_kernel.1 = (bf16[128,16,128]{2,1,0:T(8,128)(2,1)}, bf16[128,16,128]{2,1,0:T(8,128)(2,1)S(1)}) custom-call(bf16[128,48,128]{2,1,0:T(8,128)(2,1)S(1)} %all_to_all.20.in_ref), custom_call_target="tpu_custom_call" | custom-call | flops 268435456 | bytes 1572864 | tf_op jit(solution)/shard_map/mix_first_kernel/pallas_call | solution.py:212
  40.9 5.0 %all-to-all-start.1 = ((bf16[128,16,128]{2,1,0:T(8,128)(2,1)}), bf16[128,16,128]{2,1,0:T(8,128)(2,1)S(1)}, u32[]{:S(2)}, u32[]{:S(2)}) async-start(bf16[128,16,128]{2,1,0:T(8,128)(2,1)} %get-tuple-element.16), calls=%async_computation.1 | async-start | bytes 1048576 | tf_op jit(solution)/shard_map/all_to_all | solution.py:224
  45.9 0.0 copy-done
  45.9 0.0 copy-done.1
  45.9 0.0 copy-done.2
  45.9 0.0 copy-done.5
  46.0 0.0 copy-done.6
  46.0 1.1 %gate_first_kernel.1 = (bf16[4,128,512]{2,1,0:T(8,128)(2,1)S(1)}, f32[4,128,512]{2,1,0:T(8,128)S(1)}, bf16[512,128]{1,0:T(8,128)(2,1)S(1)}, bf16[128,128]{1,0:T(...) custom-call(bf16[128,16,128]{2,1,0:T(8,128)(2,1)S(1)} %get-tuple-element.17.in, ...), custom_call_target="tpu_custom_call" | custom-call | flops 134217728 | bytes 2621440 | tf_op jit(solution)/shard_map/gate_first_kernel/pallas_call | solution.py:212
  47.1 0.0 copy-start.3
  47.1 0.6 copy-done.3
  47.7 11.6 %all-to-all-done.1.mixed_ref = bf16[128,16,128]{2,1,0:T(8,128)(2,1)S(1)} async-done(((bf16[128,16,128]{2,1,0:T(8,128)(2,1)}), bf16[128,16,128]{2,1,0:T(8,128)(2,1)S(1)}, u32[]{:S(2)}, u32[]{:S(2)}) %all-to-all-start.1) | async-done | bytes 524320 | tf_op jit(solution)/shard_map/all_to_all | solution.py:224
  59.3 2.8 %middle_kernel.1 = (bf16[128,32,128]{2,1,0:T(8,128)(2,1)S(1)}, bf16[4,128,512]{2,1,0:T(8,128)(2,1)S(1)}) custom-call(bf16[128,16,128]{2,1,0:T(8,128)(2,1)S(1)} %all-to-all-done.1.mixed_ref, bf16[4,128,512]{2,1,0:T(8,128)(2,1)S(1)} %get-tuple-element.18.state_ref, f32[4,128,512]{2,1,0:T(8,128)S(1)} %get-tuple-element.19.gate_ref, ...), custom_call_target="tpu_custom_call" | custom-call | flops 335544320 | bytes 3145728 | tf_op jit(solution)/shard_map/middle_kernel/pallas_call | solution.py:212
  62.1 23.3 %all_to_all.21.in_ref = bf16[128,32,128]{2,1,0:T(8,128)(2,1)S(1)} all-to-all(bf16[128,32,128]{2,1,0:T(8,128)(2,1)S(1)} %get-tuple-element.24), channel_id=1, replica_groups=mesh['dap'=32,'rep'=4] {'dap','rep'}, dimensions={0} | all-to-all | bytes 2097152 | tf_op jit(solution)/shard_map/all_to_all | solution.py:224
  85.3 0.0 copy-start.4
  85.3 1.4 %mix_kernel.1 = bf16[128,16,128]{2,1,0:T(8,128)(2,1)} custom-call(bf16[128,32,128]{2,1,0:T(8,128)(2,1)S(1)} %all_to_all.21.in_ref), custom_call_target="tpu_custom_call" | custom-call | flops 268435456 | bytes 1572864 | tf_op jit(solution)/shard_map/mix_kernel/pallas_call | solution.py:212
  86.7 4.9 %all-to-all-start.3 = ((bf16[128,16,128]{2,1,0:T(8,128)(2,1)}), bf16[128,16,128]{2,1,0:T(8,128)(2,1)S(1)}, u32[]{:S(2)}, u32[]{:S(2)}) async-start(bf16[128,16,128]{2,1,0:T(8,128)(2,1)} %mix_kernel.1), calls=%async_computation.3 | async-start | bytes 1048576 | tf_op jit(solution)/shard_map/all_to_all | solution.py:224
  91.6 0.0 copy-done.4
  91.7 0.5 gate_second_kernel.1.gate_ref
  92.2 12.8 %all-to-all-done.3.mixed_ref = bf16[128,16,128]{2,1,0:T(8,128)(2,1)S(1)} async-done(((bf16[128,16,128]{2,1,0:T(8,128)(2,1)}), bf16[128,16,128]{2,1,0:T(8,128)(2,1)S(1)}, u32[]{:S(2)}, u32[]{:S(2)}) %all-to-all-start.3) | async-done | bytes 524320 | tf_op jit(solution)/shard_map/all_to_all | solution.py:224
  105.0 1.7 %last_kernel.1 = bf16[2048,128]{1,0:T(8,128)(2,1)} custom-call(bf16[128,16,128]{2,1,0:T(8,128)(2,1)S(1)} %all-to-all-done.3.mixed_ref, bf16[4,128,512]{2,1,0:T(8,128)(2,1)S(1)} %get-tuple-element.25.state_ref, f32[4,128,512]{2,1,0:T(8,128)S(1)} %gate_second_kernel.1.gate_ref, f32[2,128,128]{2,1,0:T(8,128)S(1)} %get-tuple-element.20.hgain_ref, ...), custom_call_target="tpu_custom_call" | custom-call | flops 67108864 | bytes 2621440 | tf_op jit(solution)/shard_map/last_kernel/pallas_call | solution.py:212
Async XLA Ops:
  39.5 6.4 %copy-start = (bf16[2,128,512]{2,1,0:T(8,128)(2,1)S(1)}, bf16[2,128,512]{2,1,0:T(8,128)(2,1)}, u32[]{:S(2)}) copy-start(bf16[2,128,512]{2,1,0:T(8,128)(2,1)} %w_ref.1) | copy-start | bytes 786436
  39.5 6.4 %copy-start.1 = (bf16[2,128,128]{2,1,0:T(8,128)(2,1)S(1)}, bf16[2,128,128]{2,1,0:T(8,128)(2,1)}, u32[]{:S(2)}) copy-start(bf16[2,128,128]{2,1,0:T(8,128)(2,1)} %g_ref.1) | copy-start | bytes 196612
  39.5 6.4 %copy-start.2 = (bf16[2,128,128]{2,1,0:T(8,128)(2,1)S(1)}, bf16[2,128,128]{2,1,0:T(8,128)(2,1)}, u32[]{:S(2)}) copy-start(bf16[2,128,128]{2,1,0:T(8,128)(2,1)} %o_ref.1) | copy-start | bytes 196612
  39.5 6.5 %copy-start.5 = (f32[2,128]{1,0:T(2,128)S(1)}, f32[2,128]{1,0:T(2,128)}, u32[]{:S(2)}) copy-start(f32[2,128]{1,0:T(2,128)} %igain_ref.1) | copy-start | bytes 3076
  39.5 6.5 %copy-start.6 = (f32[2,128]{1,0:T(2,128)S(1)}, f32[2,128]{1,0:T(2,128)}, u32[]{:S(2)}) copy-start(f32[2,128]{1,0:T(2,128)} %hgain_ref.1) | copy-start | bytes 3076
  40.9 18.4 %all-to-all-start.1 = ((bf16[128,16,128]{2,1,0:T(8,128)(2,1)}), bf16[128,16,128]{2,1,0:T(8,128)(2,1)S(1)}, u32[]{:S(2)}, u32[]{:S(2)}) async-start(bf16[128,16,128]{2,1,0:T(8,128)(2,1)} %get-tuple-element.16), calls=%async_computation.1 | async-start | bytes 1048576 | tf_op jit(solution)/shard_map/all_to_all | solution.py:224
  47.1 0.6 copy-start.3
  85.3 6.3 %copy-start.4 = (bf16[128,128]{1,0:T(8,128)(2,1)S(1)}, bf16[128,128]{1,0:T(8,128)(2,1)}, u32[]{:S(2)}) copy-start(bf16[128,128]{1,0:T(8,128)(2,1)} %copy-done.3) | copy-start | bytes 98308
  86.7 18.3 %all-to-all-start.3 = ((bf16[128,16,128]{2,1,0:T(8,128)(2,1)}), bf16[128,16,128]{2,1,0:T(8,128)(2,1)S(1)}, u32[]{:S(2)}, u32[]{:S(2)}) async-start(bf16[128,16,128]{2,1,0:T(8,128)(2,1)} %mix_kernel.1), calls=%async_computation.3 | async-start | bytes 1048576 | tf_op jit(solution)/shard_map/all_to_all | solution.py:224

commit v5 on v4

v5 whole, which is shorter than its diff:
```python
import jax
import jax.numpy as jnp
from jax import lax
from jax.experimental import pallas as pl
from jax.experimental.pallas import tpu as pltpu
from jax.sharding import PartitionSpec as P

epsilon = 1e-05
AXES = ("dap", "rep")
F32 = jnp.float32
BF16 = jnp.bfloat16
LANES = 128
ROWS = 4
VMEM_LIMIT = 24 * 1024 * 1024


def dot_nn(a, b):
    return lax.dot_general(a, b, (((1,), (0,)), ((), ())), preferred_element_type=F32)


def dot_nt(a, b):
    return lax.dot_general(a, b, (((1,), (1,)), ((), ())), preferred_element_type=F32)


def half_sigmoid(x):
    return 0.5 * jnp.tanh(x) + 0.5


def norm_lanes(x, gain):
    cen = x - jnp.mean(x, axis=1, keepdims=True)
    var = jnp.mean(cen * cen, axis=1, keepdims=True)
    return (cen * lax.rsqrt(var + epsilon) * gain).astype(BF16)


def norm_wide(x, gain_ref):
    cen = x - jnp.mean(x, axis=0, keepdims=True)
    var = jnp.mean(cen * cen, axis=0, keepdims=True)
    unit = cen * lax.rsqrt(var + epsilon)
    return jnp.concatenate(
        [
            (unit[:, c : c + LANES] * gain_ref[...]).astype(BF16)
            for c in range(0, x.shape[1], LANES)
        ],
        axis=1,
    )


def store_operands(pt, index, rows, left_s, right_s):
    ch = pt.shape[0] // 4
    chunks = pt.shape[1] // LANES
    left = half_sigmoid(pt[ch : 2 * ch]) * pt[:ch]
    right = half_sigmoid(pt[3 * ch :]) * pt[2 * ch : 3 * ch]
    for c in range(chunks):
        sl = pl.ds(c * rows + index, ch, stride=16)
        left_s[sl, :] = left[:, c * LANES : (c + 1) * LANES]
        right_s[sl, :] = right[:, c * LANES : (c + 1) * LANES]


def round_out(parts, out_ref):
    for part, ref in enumerate(parts):
        block = ref[...].reshape(out_ref.shape[0], 16, LANES)
        out_ref[:, 16 * part : 16 * (part + 1), :] = block.astype(BF16)


def flip(block, factor=1.0):
    return (block.astype(F32).T * factor).astype(BF16)


def flip_projections(w_ref, update, wt_ref):
    ch = w_ref.shape[2] // 4
    for part in range(4):
        block = w_ref[update, :, part * ch : (part + 1) * ch]
        wt_ref[part * ch : (part + 1) * ch, :] = flip(block, 0.5 if part % 2 else 1.0)


def widen(gain):
    return jnp.broadcast_to(gain, (LANES, gain.shape[1])).T


def prepare_kernel(x_hbm, w_hbm, gain_hbm, out_ref, x_ref, w_ref, gain_ref, wt_s, left_s, right_s, sem):
    rows, tokens, _ = x_ref.shape
    peers = out_ref.shape[0]
    cols = tokens // peers
    copies = [
        pltpu.make_async_copy(w_hbm.at[0:1], w_ref, sem.at[0]),
        pltpu.make_async_copy(x_hbm, x_ref, sem.at[1]),
        pltpu.make_async_copy(gain_hbm, gain_ref, sem.at[2]),
    ]
    for copy in copies:
        copy.start()
    for copy in copies:
        copy.wait()
    flip_projections(w_ref, 0, wt_s)
    for i in range(rows):
        x = x_ref[i].astype(F32)
        normed = norm_lanes(x, gain_ref[0:1, :])
        store_operands(dot_nt(wt_s[...], normed), i, rows, left_s, right_s)
    round_out((left_s, right_s), out_ref)
    state = [x_ref[i].astype(F32).reshape(peers, cols, LANES) for i in range(rows)]
    out_ref[:, 32:48, :] = jnp.concatenate(state, axis=1).astype(BF16)


def gathered(in_ref, part, rows):
    peers = in_ref.shape[0]
    block = in_ref[:, 16 * part : 16 * (part + 1), :].astype(F32)
    return jnp.concatenate(
        [
            block[:, r : r + rows, :].reshape(peers * rows, LANES).astype(BF16)
            for r in range(0, 16, rows)
        ],
        axis=1,
    )


def mix_kernel(in_ref, out_ref):
    peers = in_ref.shape[0]
    rows = ROWS
    mixed = dot_nt(gathered(in_ref, 1, rows), gathered(in_ref, 0, rows))
    blocks = [
        mixed[:, c * LANES : (c + 1) * LANES].reshape(peers, rows, LANES) for c in range(16 // rows)
    ]
    out_ref[...] = jnp.concatenate(blocks, axis=1).astype(BF16)


def mix_first_kernel(
    in_ref,
    w_ref,
    g_ref,
    o_ref,
    igain_ref,
    hgain_ref,
    out_ref,
    state_ref,
    gate_ref,
    wt_ref,
    gt_ref,
    ot_ref,
    iwide_ref,
    hwide_ref,
    wide,
):
    peers = in_ref.shape[0]
    cols, _, tokens = state_ref.shape
    wide[...] = in_ref[:, 32:48, :].astype(F32).reshape(peers * 16, LANES)
    mix_kernel(in_ref, out_ref)
    first = flip(g_ref[0], 0.5)
    for j in range(cols):
        x = wide[pl.ds(j, tokens, stride=cols), :]
        normed = norm_lanes(x, igain_ref[0:1, :])
        gate_ref[j] = half_sigmoid(dot_nt(first, normed))
        state_ref[j] = x.T.astype(BF16)
    flip_projections(w_ref, 1, wt_ref)
    gt_ref[...] = flip(g_ref[1], 0.5)
    iwide_ref[...] = widen(igain_ref[1:2, :])
    for update in range(2):
        ot_ref[update] = flip(o_ref[update])
        hwide_ref[update] = widen(hgain_ref[update : update + 1, :])


def normalize_mixed(mixed_ref, wide):
    y = mixed_ref[...].astype(F32)
    cen = y - jnp.mean(y, axis=0, keepdims=True)
    var = jnp.mean(cen * cen, axis=0, keepdims=True)
    wide[...] = (cen * lax.rsqrt(var + epsilon)).reshape(wide.shape)


def hidden_of(wide, update, j, cols, chunks, gain_ref):
    channels = gain_ref.shape[1]
    return jnp.concatenate(
        [
            (wide[pl.ds(c * cols + j, channels, stride=16), :] * gain_ref[update]).astype(BF16)
            for c in range(chunks)
        ],
        axis=1,
    )


def middle_kernel(
    mixed_ref, state_ref, gate_ref, hgain_ref, ot_ref, igain_ref, wt_ref, out_ref, next_ref, wide, left_s, right_s
):
    cols, _, tokens = state_ref.shape
    chunks = tokens // LANES
    normalize_mixed(mixed_ref, wide)
    for j in range(cols):
        update = dot_nn(ot_ref[0], hidden_of(wide, 0, j, cols, chunks, hgain_ref))
        state = (state_ref[j].astype(F32) + gate_ref[j] * update).astype(BF16)
        next_ref[j] = state
        normed = norm_wide(state.astype(F32), igain_ref)
        store_operands(dot_nn(wt_ref[...], normed), j, cols, left_s, right_s)
    round_out((left_s, right_s), out_ref)


def last_kernel(mixed_ref, state_ref, gt_ref, igain_ref, hgain_ref, ot_ref, out_ref, wide, out_s):
    cols, _, tokens = state_ref.shape
    chunks = tokens // LANES
    normalize_mixed(mixed_ref, wide)
    for j in range(cols):
        update = dot_nn(ot_ref[1], hidden_of(wide, 1, j, cols, chunks, hgain_ref))
        old = state_ref[j].astype(F32)
        gate = half_sigmoid(dot_nn(gt_ref[...], norm_wide(old, igain_ref)))
        state = (old + gate * update).astype(BF16)
        out_s[pl.ds(j, tokens, stride=cols), :] = state.T.astype(F32)
    out_ref[...] = out_s[...].astype(BF16)


def call(kernel, out_shape, scratch, flops, moved, args, limit=VMEM_LIMIT, **options):
    return pl.pallas_call(
        kernel,
        out_shape=out_shape,
        scratch_shapes=[pltpu.VMEM(*spec) if isinstance(spec, tuple) else spec for spec in scratch],
        compiler_params=pltpu.CompilerParams(vmem_limit_bytes=limit),
        cost_estimate=pl.CostEstimate(flops=flops, bytes_accessed=moved, transcendentals=0),
        name=kernel.__name__,
        **options,
    )(*args)


def exchange(buffer):
    return lax.all_to_all(buffer, AXES, split_axis=0, concat_axis=0, tiled=True)


def on_device(pair_state, input_weights, gate_weights, output_weights, input_gains, hidden_gains):
    rows, tokens, cp = pair_state.shape
    ch = output_weights.shape[1]
    peers = tokens // rows
    shape = jax.ShapeDtypeStruct
    positions = rows * tokens
    wide = ((positions, LANES), F32)
    size = positions * ch * 2
    project = 2 * positions * cp * 4 * ch
    small = 2 * positions * cp * ch
    mixing = 2 * tokens**3
    packed = shape((peers, 16, LANES), BF16)
    transposed = shape((rows, cp, tokens), BF16)

    sent = call(
        prepare_kernel,
        shape((peers, 48, LANES), BF16),
        [
            ((rows, tokens, cp), BF16),
            ((1, cp, 4 * ch), BF16),
            ((2, cp), F32),
            ((4 * ch, cp), BF16),
            wide,
            wide,
            pltpu.SemaphoreType.DMA((3,)),
        ],
        project,
        4 * size,
        args=[
            pltpu.with_memory_space_constraint(a, pltpu.HBM)
            for a in (pair_state, input_weights, input_gains)
        ],
        in_specs=[pl.BlockSpec(memory_space=pltpu.HBM)] * 3,
    )
    mixed, state, gate, wt, gt, ot, iwide, hwide = call(
        mix_first_kernel,
        (
            packed,
            transposed,
            shape((rows, cp, tokens), F32),
            shape((4 * ch, cp), BF16),
            shape((cp, cp), BF16),
            shape((2, cp, ch), BF16),
            shape((cp, LANES), F32),
            shape((2, ch, LANES), F32),
        ),
        [wide],
        mixing + 2 * small,
        7 * size,
        args=(
            exchange(sent),
            input_weights,
            gate_weights,
            output_weights,
            input_gains,
            hidden_gains,
        ),
    )
    sent, state = call(
        middle_kernel,
        (shape((peers, 32, LANES), BF16), transposed),
        [wide, wide, wide],
        project + small,
        6 * size,
        args=(exchange(mixed), state, gate, hwide, ot, iwide, wt),
    )
    mixed = call(mix_kernel, packed, [], mixing, 3 * size, args=(exchange(sent),))
    out = call(
        last_kernel,
        shape((positions, cp), BF16),
        [wide, wide],
        2 * small,
        3 * size,
        args=(exchange(mixed), state, gt, iwide, hwide, ot),
    )
    return out.reshape(tokens, rows, cp)


def solution(mesh):
    return jax.shard_map(
        on_device,
        mesh=mesh,
        in_specs=(P(AXES, None, None), P(), P(), P(), P(), P()),
        out_specs=P(None, AXES, None),
        check_vma=False,
    )
```

time: 107 us -> 105 us (0.981)
  blocking collectives: 58.9 us -> 95.1 us
  waiting for transfers between devices: 24.4 us -> 0 us
  starting transfers between devices: 9.85 us -> 0 us
  Pallas kernels: 12.9 us -> 9.49 us
    all_to_all x2 -> x4, blocking collectives: 58.9 us -> 95.1 us  [exchange(): return lax.all_to_all(buffer, AXES, split_axis=0, concat_axis=0, tiled=True)]
    all_to_all x2 -> x0, waiting for transfers between devices: 24.4 us -> none  [exchange(): return lax.all_to_all(buffer, AXES, split_axis=0, concat_axis=0, tiled=True)]
    all_to_all x2 -> x0, starting transfers between devices: 9.85 us -> none  [exchange(): return lax.all_to_all(buffer, AXES, split_axis=0, concat_axis=0, tiled=True)]
    pallas_call x7 -> x5, Pallas kernels: 12.9 us -> 9.49 us  [call(): pl.pallas_call(kernel, out_shape=out_shape, scratch_shapes=[pltpu.VMEM(*s...]
  transfers between devices with their start and end apart: 2 -> 0, of which waited for: 2 -> 0; matrix products, arithmetic and copies ran while one was open for 0% -> 0% of each run, Pallas kernels for 2% -> 0%
where the time goes in v5:
time: 105 us
  blocking collectives  95.1 us (91%)
  Pallas kernels  9.49 us (9%)
    all_to_all x4, blocking collectives, exchange(): return lax.all_to_all(buffer, AXES, split_axis=0, concat_axis=0, tiled=True)  95.1 us
    pallas_call x5, Pallas kernels, call(): pl.pallas_call(kernel, out_shape=out_shape, scratch_shapes=[pltpu.VMEM(*s...  9.49 us

profile of v5, /device:TPU:1, one launch (start us, length us, event | category | flops | bytes accessed | tf_op | source)
XLA Modules:
  0.0 104.7 jit_solution(8641181283553003146)
XLA Ops:
  0.0 2.9 %prepare_kernel.1 = bf16[128,48,128]{2,1,0:T(8,128)(2,1)S(1)} custom-call(bf16[4,512,128]{2,1,0:T(8,128)(2,1)} %x_hbm.1, bf16[2,128,512]{2,1,0:T(8,128)(2,1)} %w_ref.1, f32[2,128]{1,0:T(2,128)} %igain_ref.1), custom_call_target="tpu_custom_call" | custom-call | flops 268435456 | bytes 2097152 | tf_op jit(solution)/shard_map/prepare_kernel/pallas_call | solution.py:207
  2.9 0.0 copy-start
  3.0 0.0 copy-start.1
  3.0 0.0 copy-start.2
  3.0 0.0 copy-start.3
  3.0 0.0 copy-start.4
  3.0 35.6 %all_to_all.20.in_ref = bf16[128,48,128]{2,1,0:T(8,128)(2,1)S(1)} all-to-all(bf16[128,48,128]{2,1,0:T(8,128)(2,1)S(1)} %prepare_kernel.1), channel_id=1, replica_groups=mesh['dap'=32,'rep'=4] {'dap','rep'}, dimensions={0} | all-to-all | bytes 3145728 | tf_op jit(solution)/shard_map/all_to_all | solution.py:219
  38.6 0.0 copy-done
  38.6 0.0 copy-done.1
  38.6 0.0 copy-done.2
  38.6 0.0 copy-done.3
  38.6 0.0 copy-done.4
  38.6 1.2 %mix_first_kernel.1 = (bf16[128,16,128]{2,1,0:T(8,128)(2,1)S(1)}, bf16[4,128,512]{2,1,0:T(8,128)(2,1)S(1)}, f32[4,128,512]{2,1,0:T(8,128)S(1)}, bf16[512,128]{1,...) custom-call(bf16[128,48,128]{2,1,0:T(8,128)(2,1)S(1)} %all_to_all.20, ...), custom_call_target="tpu_custom_call" | custom-call | flops 402653184 | bytes 3670016 | tf_op jit(solution)/shard_map/mix_first_kernel/pallas_call | solution.py:207
  39.9 18.2 %all_to_all.21.mixed_ref = bf16[128,16,128]{2,1,0:T(8,128)(2,1)S(1)} all-to-all(bf16[128,16,128]{2,1,0:T(8,128)(2,1)S(1)} %get-tuple-element.15), channel_id=1, replica_groups=mesh['dap'=32,'rep'=4] {'dap','rep'}, dimensions={0} | all-to-all | bytes 1048576 | tf_op jit(solution)/shard_map/all_to_all | solution.py:219
  58.0 2.6 %middle_kernel.1 = (bf16[128,32,128]{2,1,0:T(8,128)(2,1)S(1)}, bf16[4,128,512]{2,1,0:T(8,128)(2,1)S(1)}) custom-call(bf16[128,16,128]{2,1,0:T(8,128)(2,1)S(1)} %all_to_all.21.mixed_ref, bf16[4,128,512]{2,1,0:T(8,128)(2,1)S(1)} %get-tuple-element.16.state_ref, f32[4,128,512]{2,1,0:T(8,128)S(1)} %get-tuple-element.17.gate_ref, ...), custom_call_target="tpu_custom_call" | custom-call | flops 335544320 | bytes 3145728 | tf_op jit(solution)/shard_map/middle_kernel/pallas_call | solution.py:207
  60.6 23.3 %all_to_all.22.in_ref = bf16[128,32,128]{2,1,0:T(8,128)(2,1)S(1)} all-to-all(bf16[128,32,128]{2,1,0:T(8,128)(2,1)S(1)} %get-tuple-element.22), channel_id=1, replica_groups=mesh['dap'=32,'rep'=4] {'dap','rep'}, dimensions={0} | all-to-all | bytes 2097152 | tf_op jit(solution)/shard_map/all_to_all | solution.py:219
  83.9 0.5 mix_kernel.1
  84.4 18.1 %all_to_all.23.mixed_ref = bf16[128,16,128]{2,1,0:T(8,128)(2,1)S(1)} all-to-all(bf16[128,16,128]{2,1,0:T(8,128)(2,1)S(1)} %mix_kernel.1), channel_id=1, replica_groups=mesh['dap'=32,'rep'=4] {'dap','rep'}, dimensions={0} | all-to-all | bytes 1048576 | tf_op jit(solution)/shard_map/all_to_all | solution.py:219
  102.5 2.2 %last_kernel.1 = bf16[2048,128]{1,0:T(8,128)(2,1)} custom-call(bf16[128,16,128]{2,1,0:T(8,128)(2,1)S(1)} %all_to_all.23.mixed_ref, bf16[4,128,512]{2,1,0:T(8,128)(2,1)S(1)} %get-tuple-element.23.state_ref, bf16[128,128]{1,0:T(8,128)(2,1)S(1)} %get-tuple-element.24.gt_ref, f32[128,128]{1,0:T(8,128)S(1)} %get-tuple-element.20.igain_ref, ...), custom_call_target="tpu_custom_call" | custom-call | flops 134217728 | bytes 1572864 | tf_op jit(solution)/shard_map/last_kernel/pallas_call | solution.py:207
Async XLA Ops:
  2.9 35.7 %copy-start = (bf16[2,128,512]{2,1,0:T(8,128)(2,1)S(1)}, bf16[2,128,512]{2,1,0:T(8,128)(2,1)}, u32[]{:S(2)}) copy-start(bf16[2,128,512]{2,1,0:T(8,128)(2,1)} %w_ref.1) | copy-start | bytes 786436
  3.0 35.7 %copy-start.1 = (bf16[2,128,128]{2,1,0:T(8,128)(2,1)S(1)}, bf16[2,128,128]{2,1,0:T(8,128)(2,1)}, u32[]{:S(2)}) copy-start(bf16[2,128,128]{2,1,0:T(8,128)(2,1)} %g_ref.1) | copy-start | bytes 196612
  3.0 35.6 %copy-start.2 = (bf16[2,128,128]{2,1,0:T(8,128)(2,1)S(1)}, bf16[2,128,128]{2,1,0:T(8,128)(2,1)}, u32[]{:S(2)}) copy-start(bf16[2,128,128]{2,1,0:T(8,128)(2,1)} %o_ref.1) | copy-start | bytes 196612
  3.0 35.6 %copy-start.3 = (f32[2,128]{1,0:T(2,128)S(1)}, f32[2,128]{1,0:T(2,128)}, u32[]{:S(2)}) copy-start(f32[2,128]{1,0:T(2,128)} %igain_ref.1) | copy-start | bytes 3076
  3.0 35.6 %copy-start.4 = (f32[2,128]{1,0:T(2,128)S(1)}, f32[2,128]{1,0:T(2,128)}, u32[]{:S(2)}) copy-start(f32[2,128]{1,0:T(2,128)} %hgain_ref.1) | copy-start | bytes 3076

commit v6 on v5

--- a/solution.py
+++ b/solution.py
@@ -11,6 +11,7 @@
 BF16 = jnp.bfloat16
 LANES = 128
 ROWS = 4
+PITCH = 24
 VMEM_LIMIT = 24 * 1024 * 1024
 
 
@@ -51,14 +52,14 @@
     left = half_sigmoid(pt[ch : 2 * ch]) * pt[:ch]
     right = half_sigmoid(pt[3 * ch :]) * pt[2 * ch : 3 * ch]
     for c in range(chunks):
-        sl = pl.ds(c * rows + index, ch, stride=16)
+        sl = pl.ds(c * rows + index, ch, stride=PITCH)
         left_s[sl, :] = left[:, c * LANES : (c + 1) * LANES]
         right_s[sl, :] = right[:, c * LANES : (c + 1) * LANES]
 
 
 def round_out(parts, out_ref):
     for part, ref in enumerate(parts):
-        block = ref[...].reshape(out_ref.shape[0], 16, LANES)
+        block = ref[...].reshape(out_ref.shape[0], PITCH, LANES)[:, :16, :]
         out_ref[:, 16 * part : 16 * (part + 1), :] = block.astype(BF16)
 
 
@@ -91,13 +92,12 @@
     for copy in copies:
         copy.wait()
     flip_projections(w_ref, 0, wt_s)
-    for i in range(rows):
-        x = x_ref[i].astype(F32)
-        normed = norm_lanes(x, gain_ref[0:1, :])
-        store_operands(dot_nt(wt_s[...], normed), i, rows, left_s, right_s)
-    round_out((left_s, right_s), out_ref)
+    normed = [norm_lanes(x_ref[i].astype(F32), gain_ref[0:1, :]) for i in range(rows)]
     state = [x_ref[i].astype(F32).reshape(peers, cols, LANES) for i in range(rows)]
     out_ref[:, 32:48, :] = jnp.concatenate(state, axis=1).astype(BF16)
+    for i in range(rows):
+        store_operands(dot_nt(wt_s[...], normed[i]), i, rows, left_s, right_s)
+    round_out((left_s, right_s), out_ref)
 
 
 def gathered(in_ref, part, rows):
@@ -161,15 +161,16 @@
     y = mixed_ref[...].astype(F32)
     cen = y - jnp.mean(y, axis=0, keepdims=True)
     var = jnp.mean(cen * cen, axis=0, keepdims=True)
-    wide[...] = (cen * lax.rsqrt(var + epsilon)).reshape(wide.shape)
-
-
-def hidden_of(wide, update, j, cols, chunks, gain_ref):
-    channels = gain_ref.shape[1]
+    unit = cen * lax.rsqrt(var + epsilon)
+    for h in range(unit.shape[0]):
+        wide[PITCH * h : PITCH * h + 16, :] = unit[h]
+
+
+def hidden_of(wide, j, cols, chunks, gain):
     return jnp.concatenate(
         [
-            (wide[pl.ds(c * cols + j, channels, stride=16), :] * gain_ref[update]).astype(BF16)
-            for c in range(chunks)
+            (wide[pl.ds(c * cols + j, gain.shape[0], stride=PITCH), :] * gain).astype(BF16)
+            for c in chunks
         ],
         axis=1,
     )
@@ -179,28 +180,39 @@
     mixed_ref, state_ref, gate_ref, hgain_ref, ot_ref, igain_ref, wt_ref, out_ref, next_ref, wide, left_s, right_s
 ):
     cols, _, tokens = state_ref.shape
-    chunks = tokens // LANES
+    chunks = range(tokens // LANES)
     normalize_mixed(mixed_ref, wide)
+    normed = []
     for j in range(cols):
-        update = dot_nn(ot_ref[0], hidden_of(wide, 0, j, cols, chunks, hgain_ref))
+        update = dot_nn(ot_ref[0], hidden_of(wide, j, cols, chunks, hgain_ref[0]))
         state = (state_ref[j].astype(F32) + gate_ref[j] * update).astype(BF16)
         next_ref[j] = state
-        normed = norm_wide(state.astype(F32), igain_ref)
-        store_operands(dot_nn(wt_ref[...], normed), j, cols, left_s, right_s)
+        normed.append(norm_wide(state.astype(F32), igain_ref))
+    for j in range(cols):
+        store_operands(dot_nn(wt_ref[...], normed[j]), j, cols, left_s, right_s)
     round_out((left_s, right_s), out_ref)
 
 
-def last_kernel(mixed_ref, state_ref, gt_ref, igain_ref, hgain_ref, ot_ref, out_ref, wide, out_s):
+def last_kernel(mixed_ref, state_ref, gt_ref, igain_ref, hgain_ref, ot_ref, out_hbm, wide, out_s, out_b, sem):
     cols, _, tokens = state_ref.shape
-    chunks = tokens // LANES
+    parts = sem.shape[0]
+    size = tokens // parts
+    chunks = size // LANES
     normalize_mixed(mixed_ref, wide)
-    for j in range(cols):
-        update = dot_nn(ot_ref[1], hidden_of(wide, 1, j, cols, chunks, hgain_ref))
-        old = state_ref[j].astype(F32)
-        gate = half_sigmoid(dot_nn(gt_ref[...], norm_wide(old, igain_ref)))
-        state = (old + gate * update).astype(BF16)
-        out_s[pl.ds(j, tokens, stride=cols), :] = state.T.astype(F32)
-    out_ref[...] = out_s[...].astype(BF16)
+    copies = []
+    for p in range(parts):
+        for j in range(cols):
+            old = state_ref[j, :, p * size : (p + 1) * size].astype(F32)
+            hidden = hidden_of(wide, j, cols, range(p * chunks, (p + 1) * chunks), hgain_ref[1])
+            gate = half_sigmoid(dot_nn(gt_ref[...], norm_wide(old, igain_ref)))
+            state = (old + gate * dot_nn(ot_ref[1], hidden)).astype(BF16)
+            out_s[pl.ds(p * size * cols + j, size, stride=cols), :] = state.T.astype(F32)
+        block = slice(p * size * cols, (p + 1) * size * cols)
+        out_b[block, :] = out_s[block, :].astype(BF16)
+        copies.append(pltpu.make_async_copy(out_b.at[block], out_hbm.at[block], sem.at[p]))
+        copies[-1].start()
+    for copy in copies:
+        copy.wait()
 
 
 def call(kernel, out_shape, scratch, flops, moved, args, limit=VMEM_LIMIT, **options):
@@ -226,6 +238,7 @@
     shape = jax.ShapeDtypeStruct
     positions = rows * tokens
     wide = ((positions, LANES), F32)
+    pitched = ((peers * PITCH, LANES), F32)
     size = positions * ch * 2
     project = 2 * positions * cp * 4 * ch
     small = 2 * positions * cp * ch
@@ -241,8 +254,8 @@
             ((1, cp, 4 * ch), BF16),
             ((2, cp), F32),
             ((4 * ch, cp), BF16),
-            wide,
-            wide,
+            pitched,
+            pitched,
             pltpu.SemaphoreType.DMA((3,)),
         ],
         project,
@@ -280,7 +293,7 @@
     sent, state = call(
         middle_kernel,
         (shape((peers, 32, LANES), BF16), transposed),
-        [wide, wide, wide],
+        [pitched, pitched, pitched],
         project + small,
         6 * size,
         args=(exchange(mixed), state, gate, hwide, ot, iwide, wt),
@@ -289,10 +302,11 @@
     out = call(
         last_kernel,
         shape((positions, cp), BF16),
-        [wide, wide],
+        [pitched, wide, ((positions, LANES), BF16), pltpu.SemaphoreType.DMA((2,))],
         2 * small,
         3 * size,
         args=(exchange(mixed), state, gt, iwide, hwide, ot),
+        out_specs=pl.BlockSpec(memory_space=pltpu.HBM),
     )
     return out.reshape(tokens, rows, cp)
 

time: 105 us -> 104 us (level)
  Pallas kernels: 9.49 us -> 8.12 us
    pallas_call x5, Pallas kernels: 9.49 us -> 8.12 us  [call(): pl.pallas_call(kernel, out_shape=out_shape, scratch_shapes=[pltpu.VMEM(*s...]
where the time goes in v6:
time: 104 us; the launch traced here: 103 us
  blocking collectives  95.1 us (91%)
  Pallas kernels  8.12 us (8%)
    all_to_all x4, blocking collectives, exchange(): return lax.all_to_all(buffer, AXES, split_axis=0, concat_axis=0, tiled=True)  95.1 us
    pallas_call x5, Pallas kernels, call(): pl.pallas_call(kernel, out_shape=out_shape, scratch_shapes=[pltpu.VMEM(*s...  8.12 us

profile of v6, /device:TPU:1, one launch (start us, length us, event | category | flops | bytes accessed | tf_op | source)
XLA Modules:
  0.0 103.3 jit_solution(7569565730648165707)
XLA Ops:
  0.0 2.5 %prepare_kernel.1 = bf16[128,48,128]{2,1,0:T(8,128)(2,1)S(1)} custom-call(bf16[4,512,128]{2,1,0:T(8,128)(2,1)} %x_hbm.1, bf16[2,128,512]{2,1,0:T(8,128)(2,1)} %w_ref.1, f32[2,128]{1,0:T(2,128)} %igain_ref.1), custom_call_target="tpu_custom_call" | custom-call | flops 268435456 | bytes 2097152 | tf_op jit(solution)/shard_map/prepare_kernel/pallas_call | solution.py:219
  2.5 0.0 copy-start
  2.5 0.0 copy-start.1
  2.5 0.0 copy-start.2
  2.5 0.0 copy-start.3
  2.5 0.0 copy-start.4
  2.6 35.6 %all_to_all.20.in_ref = bf16[128,48,128]{2,1,0:T(8,128)(2,1)S(1)} all-to-all(bf16[128,48,128]{2,1,0:T(8,128)(2,1)S(1)} %prepare_kernel.1), channel_id=1, replica_groups=mesh['dap'=32,'rep'=4] {'dap','rep'}, dimensions={0} | all-to-all | bytes 3145728 | tf_op jit(solution)/shard_map/all_to_all | solution.py:231
  38.2 0.0 copy-done
  38.2 0.0 copy-done.1
  38.2 0.0 copy-done.2
  38.2 0.0 copy-done.3
  38.2 0.0 copy-done.4
  38.2 1.2 %mix_first_kernel.1 = (bf16[128,16,128]{2,1,0:T(8,128)(2,1)S(1)}, bf16[4,128,512]{2,1,0:T(8,128)(2,1)S(1)}, f32[4,128,512]{2,1,0:T(8,128)S(1)}, bf16[512,128]{1,...) custom-call(bf16[128,48,128]{2,1,0:T(8,128)(2,1)S(1)} %all_to_all.20, ...), custom_call_target="tpu_custom_call" | custom-call | flops 402653184 | bytes 3670016 | tf_op jit(solution)/shard_map/mix_first_kernel/pallas_call | solution.py:219
  39.4 18.2 %all_to_all.21.mixed_ref = bf16[128,16,128]{2,1,0:T(8,128)(2,1)S(1)} all-to-all(bf16[128,16,128]{2,1,0:T(8,128)(2,1)S(1)} %get-tuple-element.15), channel_id=1, replica_groups=mesh['dap'=32,'rep'=4] {'dap','rep'}, dimensions={0} | all-to-all | bytes 1048576 | tf_op jit(solution)/shard_map/all_to_all | solution.py:231
  57.6 1.8 %middle_kernel.1 = (bf16[128,32,128]{2,1,0:T(8,128)(2,1)S(1)}, bf16[4,128,512]{2,1,0:T(8,128)(2,1)S(1)}) custom-call(bf16[128,16,128]{2,1,0:T(8,128)(2,1)S(1)} %all_to_all.21.mixed_ref, bf16[4,128,512]{2,1,0:T(8,128)(2,1)S(1)} %get-tuple-element.16.state_ref, f32[4,128,512]{2,1,0:T(8,128)S(1)} %get-tuple-element.17.gate_ref, ...), custom_call_target="tpu_custom_call" | custom-call | flops 335544320 | bytes 3145728 | tf_op jit(solution)/shard_map/middle_kernel/pallas_call | solution.py:219
  59.4 23.3 %all_to_all.22.in_ref = bf16[128,32,128]{2,1,0:T(8,128)(2,1)S(1)} all-to-all(bf16[128,32,128]{2,1,0:T(8,128)(2,1)S(1)} %get-tuple-element.22), channel_id=1, replica_groups=mesh['dap'=32,'rep'=4] {'dap','rep'}, dimensions={0} | all-to-all | bytes 2097152 | tf_op jit(solution)/shard_map/all_to_all | solution.py:231
  82.7 0.5 mix_kernel.1
  83.2 18.1 %all_to_all.23.mixed_ref = bf16[128,16,128]{2,1,0:T(8,128)(2,1)S(1)} all-to-all(bf16[128,16,128]{2,1,0:T(8,128)(2,1)S(1)} %mix_kernel.1), channel_id=1, replica_groups=mesh['dap'=32,'rep'=4] {'dap','rep'}, dimensions={0} | all-to-all | bytes 1048576 | tf_op jit(solution)/shard_map/all_to_all | solution.py:231
  101.2 2.1 %last_kernel.1 = bf16[2048,128]{1,0:T(8,128)(2,1)} custom-call(bf16[128,16,128]{2,1,0:T(8,128)(2,1)S(1)} %all_to_all.23.mixed_ref, bf16[4,128,512]{2,1,0:T(8,128)(2,1)S(1)} %get-tuple-element.23.state_ref, bf16[128,128]{1,0:T(8,128)(2,1)S(1)} %get-tuple-element.24.gt_ref, f32[128,128]{1,0:T(8,128)S(1)} %get-tuple-element.20.igain_ref, ...), custom_call_target="tpu_custom_call" | custom-call | flops 134217728 | bytes 1572864 | tf_op jit(solution)/shard_map/last_kernel/pallas_call | solution.py:219
Async XLA Ops:
  2.5 35.7 %copy-start = (bf16[2,128,512]{2,1,0:T(8,128)(2,1)S(1)}, bf16[2,128,512]{2,1,0:T(8,128)(2,1)}, u32[]{:S(2)}) copy-start(bf16[2,128,512]{2,1,0:T(8,128)(2,1)} %w_ref.1) | copy-start | bytes 786436
  2.5 35.7 %copy-start.1 = (bf16[2,128,128]{2,1,0:T(8,128)(2,1)S(1)}, bf16[2,128,128]{2,1,0:T(8,128)(2,1)}, u32[]{:S(2)}) copy-start(bf16[2,128,128]{2,1,0:T(8,128)(2,1)} %g_ref.1) | copy-start | bytes 196612
  2.5 35.6 %copy-start.2 = (bf16[2,128,128]{2,1,0:T(8,128)(2,1)S(1)}, bf16[2,128,128]{2,1,0:T(8,128)(2,1)}, u32[]{:S(2)}) copy-start(bf16[2,128,128]{2,1,0:T(8,128)(2,1)} %o_ref.1) | copy-start | bytes 196612
  2.5 35.6 %copy-start.3 = (f32[2,128]{1,0:T(2,128)S(1)}, f32[2,128]{1,0:T(2,128)}, u32[]{:S(2)}) copy-start(f32[2,128]{1,0:T(2,128)} %igain_ref.1) | copy-start | bytes 3076
  2.5 35.6 %copy-start.4 = (f32[2,128]{1,0:T(2,128)S(1)}, f32[2,128]{1,0:T(2,128)}, u32[]{:S(2)}) copy-start(f32[2,128]{1,0:T(2,128)} %hgain_ref.1) | copy-start | bytes 3076

commit v7 on v6

--- a/solution.py
+++ b/solution.py
@@ -25,12 +25,6 @@
 
 def half_sigmoid(x):
     return 0.5 * jnp.tanh(x) + 0.5
-
-
-def norm_lanes(x, gain):
-    cen = x - jnp.mean(x, axis=1, keepdims=True)
-    var = jnp.mean(cen * cen, axis=1, keepdims=True)
-    return (cen * lax.rsqrt(var + epsilon) * gain).astype(BF16)
 
 
 def norm_wide(x, gain_ref):
@@ -78,7 +72,7 @@
     return jnp.broadcast_to(gain, (LANES, gain.shape[1])).T
 
 
-def prepare_kernel(x_hbm, w_hbm, gain_hbm, out_ref, x_ref, w_ref, gain_ref, wt_s, left_s, right_s, sem):
+def prepare_kernel(x_hbm, w_hbm, gain_hbm, out_ref, x_ref, w_ref, gain_ref, wt_s, wide_s, left_s, right_s, sem):
     rows, tokens, _ = x_ref.shape
     peers = out_ref.shape[0]
     cols = tokens // peers
@@ -92,11 +86,12 @@
     for copy in copies:
         copy.wait()
     flip_projections(w_ref, 0, wt_s)
-    normed = [norm_lanes(x_ref[i].astype(F32), gain_ref[0:1, :]) for i in range(rows)]
+    wide_s[...] = widen(gain_ref[0:1, :])
+    normed = [norm_wide(x_ref[i].T.astype(F32), wide_s) for i in range(rows)]
     state = [x_ref[i].astype(F32).reshape(peers, cols, LANES) for i in range(rows)]
     out_ref[:, 32:48, :] = jnp.concatenate(state, axis=1).astype(BF16)
     for i in range(rows):
-        store_operands(dot_nt(wt_s[...], normed[i]), i, rows, left_s, right_s)
+        store_operands(dot_nn(wt_s[...], normed[i]), i, rows, left_s, right_s)
     round_out((left_s, right_s), out_ref)
 
 
@@ -138,17 +133,21 @@
     iwide_ref,
     hwide_ref,
     wide,
+    first_s,
 ):
     peers = in_ref.shape[0]
     cols, _, tokens = state_ref.shape
     wide[...] = in_ref[:, 32:48, :].astype(F32).reshape(peers * 16, LANES)
     mix_kernel(in_ref, out_ref)
     first = flip(g_ref[0], 0.5)
+    first_s[...] = widen(igain_ref[0:1, :])
+    normed = []
     for j in range(cols):
-        x = wide[pl.ds(j, tokens, stride=cols), :]
-        normed = norm_lanes(x, igain_ref[0:1, :])
-        gate_ref[j] = half_sigmoid(dot_nt(first, normed))
-        state_ref[j] = x.T.astype(BF16)
+        state = wide[pl.ds(j, tokens, stride=cols), :].astype(BF16).T
+        state_ref[j] = state
+        normed.append(norm_wide(state.astype(F32), first_s))
+    for j in range(cols):
+        gate_ref[j] = half_sigmoid(dot_nn(first, normed[j]))
     flip_projections(w_ref, 1, wt_ref)
     gt_ref[...] = flip(g_ref[1], 0.5)
     iwide_ref[...] = widen(igain_ref[1:2, :])
@@ -254,6 +253,7 @@
             ((1, cp, 4 * ch), BF16),
             ((2, cp), F32),
             ((4 * ch, cp), BF16),
+            ((cp, LANES), F32),
             pitched,
             pitched,
             pltpu.SemaphoreType.DMA((3,)),
@@ -278,7 +278,7 @@
             shape((cp, LANES), F32),
             shape((2, ch, LANES), F32),
         ),
-        [wide],
+        [wide, ((cp, LANES), F32)],
         mixing + 2 * small,
         7 * size,
         args=(

time: 104 us -> 103 us (level)
  no operation moved by 1% of the time
where the time goes in v7:
time: 103 us
  blocking collectives  95.1 us (92%)
  Pallas kernels  7.84 us (8%)
    all_to_all x4, blocking collectives, exchange(): return lax.all_to_all(buffer, AXES, split_axis=0, concat_axis=0, tiled=True)  95.1 us
    pallas_call x5, Pallas kernels, call(): pl.pallas_call(kernel, out_shape=out_shape, scratch_shapes=[pltpu.VMEM(*s...  7.84 us

profile of v7, /device:TPU:1, one launch (start us, length us, event | category | flops | bytes accessed | tf_op | source)
XLA Modules:
  0.0 103.1 jit_solution(9867648688718190225)
XLA Ops:
  0.0 2.4 %prepare_kernel.1 = bf16[128,48,128]{2,1,0:T(8,128)(2,1)S(1)} custom-call(bf16[4,512,128]{2,1,0:T(8,128)(2,1)} %x_hbm.1, bf16[2,128,512]{2,1,0:T(8,128)(2,1)} %w_ref.1, f32[2,128]{1,0:T(2,128)} %igain_ref.1), custom_call_target="tpu_custom_call" | custom-call | flops 268435456 | bytes 2097152 | tf_op jit(solution)/shard_map/prepare_kernel/pallas_call | solution.py:218
  2.4 0.0 copy-start
  2.4 0.0 copy-start.1
  2.4 0.0 copy-start.2
  2.4 0.0 copy-start.3
  2.5 0.0 copy-start.4
  2.5 35.6 %all_to_all.20.in_ref = bf16[128,48,128]{2,1,0:T(8,128)(2,1)S(1)} all-to-all(bf16[128,48,128]{2,1,0:T(8,128)(2,1)S(1)} %prepare_kernel.1), channel_id=1, replica_groups=mesh['dap'=32,'rep'=4] {'dap','rep'}, dimensions={0} | all-to-all | bytes 3145728 | tf_op jit(solution)/shard_map/all_to_all | solution.py:230
  38.1 0.0 copy-done
  38.1 0.0 copy-done.1
  38.1 0.0 copy-done.2
  38.1 0.0 copy-done.3
  38.1 0.0 copy-done.4
  38.1 1.0 %mix_first_kernel.1 = (bf16[128,16,128]{2,1,0:T(8,128)(2,1)S(1)}, bf16[4,128,512]{2,1,0:T(8,128)(2,1)S(1)}, f32[4,128,512]{2,1,0:T(8,128)S(1)}, bf16[512,128]{1,...) custom-call(bf16[128,48,128]{2,1,0:T(8,128)(2,1)S(1)} %all_to_all.20, ...), custom_call_target="tpu_custom_call" | custom-call | flops 402653184 | bytes 3670016 | tf_op jit(solution)/shard_map/mix_first_kernel/pallas_call | solution.py:218
  39.1 18.2 %all_to_all.21.mixed_ref = bf16[128,16,128]{2,1,0:T(8,128)(2,1)S(1)} all-to-all(bf16[128,16,128]{2,1,0:T(8,128)(2,1)S(1)} %get-tuple-element.15), channel_id=1, replica_groups=mesh['dap'=32,'rep'=4] {'dap','rep'}, dimensions={0} | all-to-all | bytes 1048576 | tf_op jit(solution)/shard_map/all_to_all | solution.py:230
  57.3 1.8 %middle_kernel.1 = (bf16[128,32,128]{2,1,0:T(8,128)(2,1)S(1)}, bf16[4,128,512]{2,1,0:T(8,128)(2,1)S(1)}) custom-call(bf16[128,16,128]{2,1,0:T(8,128)(2,1)S(1)} %all_to_all.21.mixed_ref, bf16[4,128,512]{2,1,0:T(8,128)(2,1)S(1)} %get-tuple-element.16.state_ref, f32[4,128,512]{2,1,0:T(8,128)S(1)} %get-tuple-element.17.gate_ref, ...), custom_call_target="tpu_custom_call" | custom-call | flops 335544320 | bytes 3145728 | tf_op jit(solution)/shard_map/middle_kernel/pallas_call | solution.py:218
  59.1 23.3 %all_to_all.22.in_ref = bf16[128,32,128]{2,1,0:T(8,128)(2,1)S(1)} all-to-all(bf16[128,32,128]{2,1,0:T(8,128)(2,1)S(1)} %get-tuple-element.22), channel_id=1, replica_groups=mesh['dap'=32,'rep'=4] {'dap','rep'}, dimensions={0} | all-to-all | bytes 2097152 | tf_op jit(solution)/shard_map/all_to_all | solution.py:230
  82.4 0.5 mix_kernel.1
  82.9 18.1 %all_to_all.23.mixed_ref = bf16[128,16,128]{2,1,0:T(8,128)(2,1)S(1)} all-to-all(bf16[128,16,128]{2,1,0:T(8,128)(2,1)S(1)} %mix_kernel.1), channel_id=1, replica_groups=mesh['dap'=32,'rep'=4] {'dap','rep'}, dimensions={0} | all-to-all | bytes 1048576 | tf_op jit(solution)/shard_map/all_to_all | solution.py:230
  101.0 2.1 %last_kernel.1 = bf16[2048,128]{1,0:T(8,128)(2,1)} custom-call(bf16[128,16,128]{2,1,0:T(8,128)(2,1)S(1)} %all_to_all.23.mixed_ref, bf16[4,128,512]{2,1,0:T(8,128)(2,1)S(1)} %get-tuple-element.23.state_ref, bf16[128,128]{1,0:T(8,128)(2,1)S(1)} %get-tuple-element.24.gt_ref, f32[128,128]{1,0:T(8,128)S(1)} %get-tuple-element.20.igain_ref, ...), custom_call_target="tpu_custom_call" | custom-call | flops 134217728 | bytes 1572864 | tf_op jit(solution)/shard_map/last_kernel/pallas_call | solution.py:218
Async XLA Ops:
  2.4 35.7 %copy-start = (bf16[2,128,512]{2,1,0:T(8,128)(2,1)S(1)}, bf16[2,128,512]{2,1,0:T(8,128)(2,1)}, u32[]{:S(2)}) copy-start(bf16[2,128,512]{2,1,0:T(8,128)(2,1)} %w_ref.1) | copy-start | bytes 786436
  2.4 35.7 %copy-start.1 = (bf16[2,128,128]{2,1,0:T(8,128)(2,1)S(1)}, bf16[2,128,128]{2,1,0:T(8,128)(2,1)}, u32[]{:S(2)}) copy-start(bf16[2,128,128]{2,1,0:T(8,128)(2,1)} %g_ref.1) | copy-start | bytes 196612
  2.4 35.6 %copy-start.2 = (bf16[2,128,128]{2,1,0:T(8,128)(2,1)S(1)}, bf16[2,128,128]{2,1,0:T(8,128)(2,1)}, u32[]{:S(2)}) copy-start(bf16[2,128,128]{2,1,0:T(8,128)(2,1)} %o_ref.1) | copy-start | bytes 196612
  2.4 35.6 %copy-start.3 = (f32[2,128]{1,0:T(2,128)S(1)}, f32[2,128]{1,0:T(2,128)}, u32[]{:S(2)}) copy-start(f32[2,128]{1,0:T(2,128)} %igain_ref.1) | copy-start | bytes 3076
  2.5 35.6 %copy-start.4 = (f32[2,128]{1,0:T(2,128)S(1)}, f32[2,128]{1,0:T(2,128)}, u32[]{:S(2)}) copy-start(f32[2,128]{1,0:T(2,128)} %hgain_ref.1) | copy-start | bytes 3076

commit v8 on v7

--- a/solution.py
+++ b/solution.py
@@ -176,7 +176,7 @@
 
 
 def middle_kernel(
-    mixed_ref, state_ref, gate_ref, hgain_ref, ot_ref, igain_ref, wt_ref, out_ref, next_ref, wide, left_s, right_s
+    mixed_ref, state_ref, gate_ref, hgain_ref, ot_ref, igain_ref, wt_ref, gt_ref, out_ref, next_ref, next_gate_ref, wide, left_s, right_s
 ):
     cols, _, tokens = state_ref.shape
     chunks = range(tokens // LANES)
@@ -189,10 +189,11 @@
         normed.append(norm_wide(state.astype(F32), igain_ref))
     for j in range(cols):
         store_operands(dot_nn(wt_ref[...], normed[j]), j, cols, left_s, right_s)
+        next_gate_ref[j] = half_sigmoid(dot_nn(gt_ref[...], normed[j]))
     round_out((left_s, right_s), out_ref)
 
 
-def last_kernel(mixed_ref, state_ref, gt_ref, igain_ref, hgain_ref, ot_ref, out_hbm, wide, out_s, out_b, sem):
+def last_kernel(mixed_ref, state_ref, gate_ref, hgain_ref, ot_ref, out_hbm, wide, out_s, out_b, sem):
     cols, _, tokens = state_ref.shape
     parts = sem.shape[0]
     size = tokens // parts
@@ -201,10 +202,10 @@
     copies = []
     for p in range(parts):
         for j in range(cols):
-            old = state_ref[j, :, p * size : (p + 1) * size].astype(F32)
+            lanes = slice(p * size, (p + 1) * size)
             hidden = hidden_of(wide, j, cols, range(p * chunks, (p + 1) * chunks), hgain_ref[1])
-            gate = half_sigmoid(dot_nn(gt_ref[...], norm_wide(old, igain_ref)))
-            state = (old + gate * dot_nn(ot_ref[1], hidden)).astype(BF16)
+            update = dot_nn(ot_ref[1], hidden)
+            state = (state_ref[j, :, lanes].astype(F32) + gate_ref[j, :, lanes] * update).astype(BF16)
             out_s[pl.ds(p * size * cols + j, size, stride=cols), :] = state.T.astype(F32)
         block = slice(p * size * cols, (p + 1) * size * cols)
         out_b[block, :] = out_s[block, :].astype(BF16)
@@ -244,6 +245,7 @@
     mixing = 2 * tokens**3
     packed = shape((peers, 16, LANES), BF16)
     transposed = shape((rows, cp, tokens), BF16)
+    gating = shape((rows, cp, tokens), F32)
 
     sent = call(
         prepare_kernel,
@@ -271,7 +273,7 @@
         (
             packed,
             transposed,
-            shape((rows, cp, tokens), F32),
+            gating,
             shape((4 * ch, cp), BF16),
             shape((cp, cp), BF16),
             shape((2, cp, ch), BF16),
@@ -290,22 +292,22 @@
             hidden_gains,
         ),
     )
-    sent, state = call(
+    sent, state, gate = call(
         middle_kernel,
-        (shape((peers, 32, LANES), BF16), transposed),
+        (shape((peers, 32, LANES), BF16), transposed, gating),
         [pitched, pitched, pitched],
-        project + small,
-        6 * size,
-        args=(exchange(mixed), state, gate, hwide, ot, iwide, wt),
+        project + 2 * small,
+        8 * size,
+        args=(exchange(mixed), state, gate, hwide, ot, iwide, wt, gt),
     )
     mixed = call(mix_kernel, packed, [], mixing, 3 * size, args=(exchange(sent),))
     out = call(
         last_kernel,
         shape((positions, cp), BF16),
         [pitched, wide, ((positions, LANES), BF16), pltpu.SemaphoreType.DMA((2,))],
-        2 * small,
-        3 * size,
-        args=(exchange(mixed), state, gt, iwide, hwide, ot),
+        small,
+        5 * size,
+        args=(exchange(mixed), state, gate, hwide, ot),
         out_specs=pl.BlockSpec(memory_space=pltpu.HBM),
     )
     return out.reshape(tokens, rows, cp)

time: 103 us -> 103 us (level)
  no operation moved by 1% of the time
where the time goes in v8:
time: 103 us
  blocking collectives  95.1 us (92%)
  Pallas kernels  7.34 us (7%)
    all_to_all x4, blocking collectives, exchange(): return lax.all_to_all(buffer, AXES, split_axis=0, concat_axis=0, tiled=True)  95.1 us
    pallas_call x5, Pallas kernels, call(): pl.pallas_call(kernel, out_shape=out_shape, scratch_shapes=[pltpu.VMEM(*s...  7.34 us

profile of v8, /device:TPU:1, one launch (start us, length us, event | category | flops | bytes accessed | tf_op | source)
XLA Modules:
  0.0 102.6 jit_solution(16381978449767642830)
XLA Ops:
  0.0 2.4 %prepare_kernel.1 = bf16[128,48,128]{2,1,0:T(8,128)(2,1)S(1)} custom-call(bf16[4,512,128]{2,1,0:T(8,128)(2,1)} %x_hbm.1, bf16[2,128,512]{2,1,0:T(8,128)(2,1)} %w_ref.1, f32[2,128]{1,0:T(2,128)} %igain_ref.1), custom_call_target="tpu_custom_call" | custom-call | flops 268435456 | bytes 2097152 | tf_op jit(solution)/shard_map/prepare_kernel/pallas_call | solution.py:219
  2.4 0.0 copy-start
  2.4 0.0 copy-start.1
  2.4 0.0 copy-start.2
  2.4 0.0 copy-start.3
  2.5 0.0 copy-start.4
  2.5 35.6 %all_to_all.20.in_ref = bf16[128,48,128]{2,1,0:T(8,128)(2,1)S(1)} all-to-all(bf16[128,48,128]{2,1,0:T(8,128)(2,1)S(1)} %prepare_kernel.1), channel_id=1, replica_groups=mesh['dap'=32,'rep'=4] {'dap','rep'}, dimensions={0} | all-to-all | bytes 3145728 | tf_op jit(solution)/shard_map/all_to_all | solution.py:231
  38.1 0.0 copy-done
  38.1 0.0 copy-done.1
  38.1 0.0 copy-done.2
  38.1 0.0 copy-done.3
  38.1 0.0 copy-done.4
  38.1 1.0 %mix_first_kernel.1 = (bf16[128,16,128]{2,1,0:T(8,128)(2,1)S(1)}, bf16[4,128,512]{2,1,0:T(8,128)(2,1)S(1)}, f32[4,128,512]{2,1,0:T(8,128)S(1)}, bf16[512,128]{1,...) custom-call(bf16[128,48,128]{2,1,0:T(8,128)(2,1)S(1)} %all_to_all.20, ...), custom_call_target="tpu_custom_call" | custom-call | flops 402653184 | bytes 3670016 | tf_op jit(solution)/shard_map/mix_first_kernel/pallas_call | solution.py:219
  39.1 18.2 %all_to_all.21.mixed_ref = bf16[128,16,128]{2,1,0:T(8,128)(2,1)S(1)} all-to-all(bf16[128,16,128]{2,1,0:T(8,128)(2,1)S(1)} %get-tuple-element.16), channel_id=1, replica_groups=mesh['dap'=32,'rep'=4] {'dap','rep'}, dimensions={0} | all-to-all | bytes 1048576 | tf_op jit(solution)/shard_map/all_to_all | solution.py:231
  57.3 1.9 %middle_kernel.1 = (bf16[128,32,128]{2,1,0:T(8,128)(2,1)S(1)}, bf16[4,128,512]{2,1,0:T(8,128)(2,1)S(1)}, f32[4,128,512]{2,1,0:T(8,128)S(1)}) custom-call(bf16[128,16,128]{2,1,0:T(8,128)(2,1)S(1)} %all_to_all.21.mixed_ref, bf16[4,128,512]{2,1,0:T(8,128)(2,1)S(1)} %get-tuple-element.17.state_ref, f32[4,128,512]{2,1,0:T(8,128)S(1)} %get-tuple-element.18.gate_ref, ...), custom_call_target="tpu_custom_call" | custom-call | flops 402653184 | bytes 4194304 | tf_op jit(solution)/shard_map/middle_kernel/pallas_call | solution.py:219
  59.2 23.3 %all_to_all.22.in_ref = bf16[128,32,128]{2,1,0:T(8,128)(2,1)S(1)} all-to-all(bf16[128,32,128]{2,1,0:T(8,128)(2,1)S(1)} %get-tuple-element.24), channel_id=1, replica_groups=mesh['dap'=32,'rep'=4] {'dap','rep'}, dimensions={0} | all-to-all | bytes 2097152 | tf_op jit(solution)/shard_map/all_to_all | solution.py:231
  82.5 0.5 mix_kernel.1
  83.0 18.1 %all_to_all.23.mixed_ref = bf16[128,16,128]{2,1,0:T(8,128)(2,1)S(1)} all-to-all(bf16[128,16,128]{2,1,0:T(8,128)(2,1)S(1)} %mix_kernel.1), channel_id=1, replica_groups=mesh['dap'=32,'rep'=4] {'dap','rep'}, dimensions={0} | all-to-all | bytes 1048576 | tf_op jit(solution)/shard_map/all_to_all | solution.py:231
  101.0 1.5 %last_kernel.1 = bf16[2048,128]{1,0:T(8,128)(2,1)} custom-call(bf16[128,16,128]{2,1,0:T(8,128)(2,1)S(1)} %all_to_all.23.mixed_ref, bf16[4,128,512]{2,1,0:T(8,128)(2,1)S(1)} %get-tuple-element.25.state_ref, f32[4,128,512]{2,1,0:T(8,128)S(1)} %get-tuple-element.26.gate_ref, f32[2,128,128]{2,1,0:T(8,128)S(1)} %get-tuple-element.19.hgain_ref, ...), custom_call_target="tpu_custom_call" | custom-call | flops 67108864 | bytes 2621440 | tf_op jit(solution)/shard_map/last_kernel/pallas_call | solution.py:219
Async XLA Ops:
  2.4 35.7 %copy-start = (bf16[2,128,512]{2,1,0:T(8,128)(2,1)S(1)}, bf16[2,128,512]{2,1,0:T(8,128)(2,1)}, u32[]{:S(2)}) copy-start(bf16[2,128,512]{2,1,0:T(8,128)(2,1)} %w_ref.1) | copy-start | bytes 786436
  2.4 35.7 %copy-start.1 = (bf16[2,128,128]{2,1,0:T(8,128)(2,1)S(1)}, bf16[2,128,128]{2,1,0:T(8,128)(2,1)}, u32[]{:S(2)}) copy-start(bf16[2,128,128]{2,1,0:T(8,128)(2,1)} %g_ref.1) | copy-start | bytes 196612
  2.4 35.6 %copy-start.2 = (bf16[2,128,128]{2,1,0:T(8,128)(2,1)S(1)}, bf16[2,128,128]{2,1,0:T(8,128)(2,1)}, u32[]{:S(2)}) copy-start(bf16[2,128,128]{2,1,0:T(8,128)(2,1)} %o_ref.1) | copy-start | bytes 196612
  2.4 35.6 %copy-start.3 = (f32[2,128]{1,0:T(2,128)S(1)}, f32[2,128]{1,0:T(2,128)}, u32[]{:S(2)}) copy-start(f32[2,128]{1,0:T(2,128)} %igain_ref.1) | copy-start | bytes 3076
  2.5 35.6 %copy-start.4 = (f32[2,128]{1,0:T(2,128)S(1)}, f32[2,128]{1,0:T(2,128)}, u32[]{:S(2)}) copy-start(f32[2,128]{1,0:T(2,128)} %hgain_ref.1) | copy-start | bytes 3076

commit v9 on v8

--- a/solution.py
+++ b/solution.py
@@ -77,16 +77,17 @@
     peers = out_ref.shape[0]
     cols = tokens // peers
     copies = [
+        pltpu.make_async_copy(gain_hbm, gain_ref, sem.at[2]),
         pltpu.make_async_copy(w_hbm.at[0:1], w_ref, sem.at[0]),
         pltpu.make_async_copy(x_hbm, x_ref, sem.at[1]),
-        pltpu.make_async_copy(gain_hbm, gain_ref, sem.at[2]),
     ]
     for copy in copies:
         copy.start()
-    for copy in copies:
-        copy.wait()
+    copies[0].wait()
+    wide_s[...] = widen(gain_ref[0:1, :])
+    copies[1].wait()
     flip_projections(w_ref, 0, wt_s)
-    wide_s[...] = widen(gain_ref[0:1, :])
+    copies[2].wait()
     normed = [norm_wide(x_ref[i].T.astype(F32), wide_s) for i in range(rows)]
     state = [x_ref[i].astype(F32).reshape(peers, cols, LANES) for i in range(rows)]
     out_ref[:, 32:48, :] = jnp.concatenate(state, axis=1).astype(BF16)
@@ -126,32 +127,23 @@
     hgain_ref,
     out_ref,
     state_ref,
-    gate_ref,
     wt_ref,
     gt_ref,
     ot_ref,
     iwide_ref,
     hwide_ref,
     wide,
-    first_s,
 ):
     peers = in_ref.shape[0]
     cols, _, tokens = state_ref.shape
     wide[...] = in_ref[:, 32:48, :].astype(F32).reshape(peers * 16, LANES)
     mix_kernel(in_ref, out_ref)
-    first = flip(g_ref[0], 0.5)
-    first_s[...] = widen(igain_ref[0:1, :])
-    normed = []
     for j in range(cols):
-        state = wide[pl.ds(j, tokens, stride=cols), :].astype(BF16).T
-        state_ref[j] = state
-        normed.append(norm_wide(state.astype(F32), first_s))
-    for j in range(cols):
-        gate_ref[j] = half_sigmoid(dot_nn(first, normed[j]))
+        state_ref[j] = wide[pl.ds(j, tokens, stride=cols), :].astype(BF16).T
     flip_projections(w_ref, 1, wt_ref)
-    gt_ref[...] = flip(g_ref[1], 0.5)
-    iwide_ref[...] = widen(igain_ref[1:2, :])
     for update in range(2):
+        gt_ref[update] = flip(g_ref[update], 0.5)
+        iwide_ref[update] = widen(igain_ref[update : update + 1, :])
         ot_ref[update] = flip(o_ref[update])
         hwide_ref[update] = widen(hgain_ref[update : update + 1, :])
 
@@ -176,7 +168,7 @@
 
 
 def middle_kernel(
-    mixed_ref, state_ref, gate_ref, hgain_ref, ot_ref, igain_ref, wt_ref, gt_ref, out_ref, next_ref, next_gate_ref, wide, left_s, right_s
+    mixed_ref, state_ref, hgain_ref, ot_ref, igain_ref, wt_ref, gt_ref, out_ref, next_ref, next_gate_ref, wide, left_s, right_s
 ):
     cols, _, tokens = state_ref.shape
     chunks = range(tokens // LANES)
@@ -184,12 +176,14 @@
     normed = []
     for j in range(cols):
         update = dot_nn(ot_ref[0], hidden_of(wide, j, cols, chunks, hgain_ref[0]))
-        state = (state_ref[j].astype(F32) + gate_ref[j] * update).astype(BF16)
+        old = state_ref[j].astype(F32)
+        gate = half_sigmoid(dot_nn(gt_ref[0], norm_wide(old, igain_ref.at[0])))
+        state = (old + gate * update).astype(BF16)
         next_ref[j] = state
-        normed.append(norm_wide(state.astype(F32), igain_ref))
+        normed.append(norm_wide(state.astype(F32), igain_ref.at[1]))
     for j in range(cols):
         store_operands(dot_nn(wt_ref[...], normed[j]), j, cols, left_s, right_s)
-        next_gate_ref[j] = half_sigmoid(dot_nn(gt_ref[...], normed[j]))
+        next_gate_ref[j] = half_sigmoid(dot_nn(gt_ref[1], normed[j]))
     round_out((left_s, right_s), out_ref)
 
 
@@ -268,21 +262,20 @@
         ],
         in_specs=[pl.BlockSpec(memory_space=pltpu.HBM)] * 3,
     )
-    mixed, state, gate, wt, gt, ot, iwide, hwide = call(
+    mixed, state, wt, gt, ot, iwide, hwide = call(
         mix_first_kernel,
         (
             packed,
             transposed,
-            gating,
             shape((4 * ch, cp), BF16),
-            shape((cp, cp), BF16),
+            shape((2, cp, cp), BF16),
             shape((2, cp, ch), BF16),
-            shape((cp, LANES), F32),
+            shape((2, cp, LANES), F32),
             shape((2, ch, LANES), F32),
         ),
-        [wide, ((cp, LANES), F32)],
-        mixing + 2 * small,
-        7 * size,
+        [wide],
+        mixing,
+        5 * size,
         args=(
             exchange(sent),
             input_weights,
@@ -296,15 +289,15 @@
         middle_kernel,
         (shape((peers, 32, LANES), BF16), transposed, gating),
         [pitched, pitched, pitched],
-        project + 2 * small,
+        project + 3 * small,
         8 * size,
-        args=(exchange(mixed), state, gate, hwide, ot, iwide, wt, gt),
+        args=(exchange(mixed), state, hwide, ot, iwide, wt, gt),
     )
     mixed = call(mix_kernel, packed, [], mixing, 3 * size, args=(exchange(sent),))
     out = call(
         last_kernel,
         shape((positions, cp), BF16),
-        [pitched, wide, ((positions, LANES), BF16), pltpu.SemaphoreType.DMA((2,))],
+        [pitched, wide, ((positions, LANES), BF16), pltpu.SemaphoreType.DMA((4,))],
         small,
         5 * size,
         args=(exchange(mixed), state, gate, hwide, ot),

time: 103 us -> 103 us (level)
  no operation moved by 1% of the time
where the time goes in v9:
time: 103 us; the launch traced here: 102 us
  blocking collectives  95.1 us (92%)
  Pallas kernels  7.19 us (7%)
    all_to_all x4, blocking collectives, exchange(): return lax.all_to_all(buffer, AXES, split_axis=0, concat_axis=0, tiled=True)  95.1 us
    pallas_call x5, Pallas kernels, call(): pl.pallas_call(kernel, out_shape=out_shape, scratch_shapes=[pltpu.VMEM(*s...  7.19 us

profile of v9, /device:TPU:1, one launch (start us, length us, event | category | flops | bytes accessed | tf_op | source)
XLA Modules:
  0.0 102.4 jit_solution(17312939785762151242)
XLA Ops:
  0.0 2.3 %prepare_kernel.1 = bf16[128,48,128]{2,1,0:T(8,128)(2,1)S(1)} custom-call(bf16[4,512,128]{2,1,0:T(8,128)(2,1)} %x_hbm.1, bf16[2,128,512]{2,1,0:T(8,128)(2,1)} %w_ref.1, f32[2,128]{1,0:T(2,128)} %igain_ref.1), custom_call_target="tpu_custom_call" | custom-call | flops 268435456 | bytes 2097152 | tf_op jit(solution)/shard_map/prepare_kernel/pallas_call | solution.py:213
  2.3 0.0 copy-start
  2.3 0.0 copy-start.1
  2.4 0.0 copy-start.2
  2.4 0.0 copy-start.3
  2.4 0.0 copy-start.4
  2.4 35.6 %all_to_all.20.in_ref = bf16[128,48,128]{2,1,0:T(8,128)(2,1)S(1)} all-to-all(bf16[128,48,128]{2,1,0:T(8,128)(2,1)S(1)} %prepare_kernel.1), channel_id=1, replica_groups=mesh['dap'=32,'rep'=4] {'dap','rep'}, dimensions={0} | all-to-all | bytes 3145728 | tf_op jit(solution)/shard_map/all_to_all | solution.py:225
  38.0 0.0 copy-done
  38.0 0.0 copy-done.1
  38.0 0.0 copy-done.2
  38.0 0.0 copy-done.3
  38.0 0.0 copy-done.4
  38.0 0.5 mix_first_kernel.1
  38.6 18.2 %all_to_all.21.mixed_ref = bf16[128,16,128]{2,1,0:T(8,128)(2,1)S(1)} all-to-all(bf16[128,16,128]{2,1,0:T(8,128)(2,1)S(1)} %get-tuple-element.15), channel_id=1, replica_groups=mesh['dap'=32,'rep'=4] {'dap','rep'}, dimensions={0} | all-to-all | bytes 1048576 | tf_op jit(solution)/shard_map/all_to_all | solution.py:225
  56.7 2.3 %middle_kernel.1 = (bf16[128,32,128]{2,1,0:T(8,128)(2,1)S(1)}, bf16[4,128,512]{2,1,0:T(8,128)(2,1)S(1)}, f32[4,128,512]{2,1,0:T(8,128)S(1)}) custom-call(bf16[128,16,128]{2,1,0:T(8,128)(2,1)S(1)} %all_to_all.21.mixed_ref, bf16[4,128,512]{2,1,0:T(8,128)(2,1)S(1)} %get-tuple-element.16.state_ref, f32[2,128,128]{2,1,0:T(8,128)S(1)} %get-tuple-element.17.hgain_ref, ...), custom_call_target="tpu_custom_call" | custom-call | flops 469762048 | bytes 4194304 | tf_op jit(solution)/shard_map/middle_kernel/pallas_call | solution.py:213
  59.0 23.3 %all_to_all.22.in_ref = bf16[128,32,128]{2,1,0:T(8,128)(2,1)S(1)} all-to-all(bf16[128,32,128]{2,1,0:T(8,128)(2,1)S(1)} %get-tuple-element.22), channel_id=1, replica_groups=mesh['dap'=32,'rep'=4] {'dap','rep'}, dimensions={0} | all-to-all | bytes 2097152 | tf_op jit(solution)/shard_map/all_to_all | solution.py:225
  82.3 0.5 mix_kernel.1
  82.8 18.1 %all_to_all.23.mixed_ref = bf16[128,16,128]{2,1,0:T(8,128)(2,1)S(1)} all-to-all(bf16[128,16,128]{2,1,0:T(8,128)(2,1)S(1)} %mix_kernel.1), channel_id=1, replica_groups=mesh['dap'=32,'rep'=4] {'dap','rep'}, dimensions={0} | all-to-all | bytes 1048576 | tf_op jit(solution)/shard_map/all_to_all | solution.py:225
  100.9 1.5 %last_kernel.1 = bf16[2048,128]{1,0:T(8,128)(2,1)} custom-call(bf16[128,16,128]{2,1,0:T(8,128)(2,1)S(1)} %all_to_all.23.mixed_ref, bf16[4,128,512]{2,1,0:T(8,128)(2,1)S(1)} %get-tuple-element.23.state_ref, f32[4,128,512]{2,1,0:T(8,128)S(1)} %get-tuple-element.24.gate_ref, f32[2,128,128]{2,1,0:T(8,128)S(1)} %get-tuple-element.17.hgain_ref, ...), custom_call_target="tpu_custom_call" | custom-call | flops 67108864 | bytes 2621440 | tf_op jit(solution)/shard_map/last_kernel/pallas_call | solution.py:213
Async XLA Ops:
  2.3 35.7 %copy-start = (bf16[2,128,512]{2,1,0:T(8,128)(2,1)S(1)}, bf16[2,128,512]{2,1,0:T(8,128)(2,1)}, u32[]{:S(2)}) copy-start(bf16[2,128,512]{2,1,0:T(8,128)(2,1)} %w_ref.1) | copy-start | bytes 786436
  2.3 35.7 %copy-start.1 = (bf16[2,128,128]{2,1,0:T(8,128)(2,1)S(1)}, bf16[2,128,128]{2,1,0:T(8,128)(2,1)}, u32[]{:S(2)}) copy-start(bf16[2,128,128]{2,1,0:T(8,128)(2,1)} %g_ref.1) | copy-start | bytes 196612
  2.4 35.6 %copy-start.2 = (bf16[2,128,128]{2,1,0:T(8,128)(2,1)S(1)}, bf16[2,128,128]{2,1,0:T(8,128)(2,1)}, u32[]{:S(2)}) copy-start(bf16[2,128,128]{2,1,0:T(8,128)(2,1)} %o_ref.1) | copy-start | bytes 196612
  2.4 35.6 %copy-start.3 = (f32[2,128]{1,0:T(2,128)S(1)}, f32[2,128]{1,0:T(2,128)}, u32[]{:S(2)}) copy-start(f32[2,128]{1,0:T(2,128)} %igain_ref.1) | copy-start | bytes 3076
  2.4 35.6 %copy-start.4 = (f32[2,128]{1,0:T(2,128)S(1)}, f32[2,128]{1,0:T(2,128)}, u32[]{:S(2)}) copy-start(f32[2,128]{1,0:T(2,128)} %hgain_ref.1) | copy-start | bytes 3076
